TPU v7x, 32 devices: a whole 2x2x4 slice. The times are simulated.
32 devices in a mesh: gy: 8 (over z, y), gz: 4 (over x, core).
Axes of the slice: x: 2, y: 2, z: 4, core: 2. Of those that a mesh axis runs over, the one named last changes fastest.
Arguments:
- thermal_state: float32 [32, 1024, 512], P(None, 'gy', 'gz'), may hold values from -6 to 6
- fourier_ratio_width: float32 [32], replicated, may hold values from 50 to 5000
- fourier_ratio_height: float32 [32], replicated, may hold values from 50 to 5000
Outputs:
- stepped: float32 [32, 1024, 512], P(None, 'gy', 'gz')
All inputs are finite; a program needn't handle non-finite values.
Results may differ from a plain program's by a relative error of at most 0.0005.
Values sent between devices are 32-bit elements; how exact they have to be, the bound alone decides.
No kernel may reach another device: no remote copies, remote signals or barrier semaphores. Data moves between devices by JAX's collectives and lax.ppermute only.
A program may use at most 128 MiB of HBM per device.

v0:
```python
import functools

import jax
import jax.numpy as jnp
from jax import lax
from jax.experimental import pallas as pl
from jax.experimental.pallas import tpu as pltpu
from jax.sharding import PartitionSpec as P

alpha = 2.0 / 11.0
inner_weight = 12.0 / 11.0
outer_weight = 3.0 / 44.0
F32 = jnp.float32
BF16 = jnp.bfloat16
STEPS = 4
VMEM = 24 * 1024 * 1024


def spread(rates, table):
    for k in range(table.shape[0]):
        table[pl.ds(k, 1), :] = jnp.full((1, table.shape[1]), rates[k], F32)


class Line:
    def __init__(self, rate, position, devices, m):
        beside = inner_weight * rate - alpha
        eps = (1.0 + 2.0 * alpha) / (2.0 * beside)
        sinh = jnp.sqrt(eps * (2.0 + eps))
        corner = rate * outer_weight
        self.m = m
        self.theta = jnp.log1p(eps + sinh)
        total = m * devices
        self.far = total + 1 - m * position
        self.near = m * position
        self.c = m // 2
        self.green = 1.0 / (2.0 * beside * sinh * (1.0 - self.power(2 * (total + 1))))
        self.rho = 1.0 + 2.0 * alpha * (1.0 + eps) + 4.0 * corner * eps * (2.0 + eps)
        self.side = -corner / beside
        self.mid = 2.0 * self.side * (1.0 + eps) - alpha / beside
        self.corner = corner
        self.is_first = jnp.where(position == 0, 1.0, 0.0).astype(F32)
        self.is_last = jnp.where(position == devices - 1, 1.0, 0.0).astype(F32)
        self.cell = lax.broadcasted_iota(jnp.int32, rate.shape, 1)

    def power(self, n):
        return jnp.exp(-self.theta * jnp.asarray(n, F32))

    def vectors(self):
        i = (self.cell + (1 - self.c)).astype(F32)
        down, up = jnp.exp(-self.theta * i), jnp.exp(self.theta * i)
        self.cut_far = self.power(2 * (self.far - self.c))
        self.cut_near = self.power(2 * (self.near + self.c))
        self.phi = down - self.cut_far * up
        self.chi = up - self.cut_near * down
        self.ends = jnp.where(self.cell == 0, self.is_first, 0.0) + jnp.where(
            self.cell == self.m - 1, self.is_last, 0.0
        )
        self.weight = self.green * (self.rho + self.corner * self.ends)
        self.send_up = self.weight * self.chi * self.power(self.m - self.c)
        self.send_down = self.weight * self.phi * self.power(self.c - 1)
        self.get_up = self.phi * self.power(self.c)
        self.get_down = self.chi * self.power(self.m + 1 - self.c)
        self.head = jnp.where(self.cell == 0, 1.0, 0.0).astype(F32)
        self.tail = jnp.where(self.cell == self.m - 1, 1.0, 0.0).astype(F32)


def split(a):
    hi = a.astype(BF16)
    return hi, (a - hi.astype(F32)).astype(BF16)


def dot(a, b, ca, cb):
    return lax.dot_general(a, b, (((ca,), (cb,)), ((), ())), preferred_element_type=F32)


def moments_kernel(devices, rates, x, out, table, eighth, up_rows, down_rows, ends):
    step = pl.program_id(0)
    group, m = x.shape[0], x.shape[1]
    planes = table.shape[0]
    position = lax.axis_index("gy")

    @pl.when(step == 0)
    def _():
        spread(rates, table)
        eighth[...] = Line(table[...], position, devices, m).power(8)

    for g in range(group):
        k = step * group + g
        ratio = jnp.broadcast_to(eighth[pl.ds(k, 1), :], (8, x.shape[2]))
        up, down = x[g, 0:8, :], x[g, m - 8 : m, :]
        for v in range(1, m // 8):
            up = up * ratio + x[g, 8 * v : 8 * v + 8, :]
            w = m - 8 - 8 * v
            down = down * ratio + x[g, w : w + 8, :]
        up_rows[pl.ds(k, 1)] = up[None]
        down_rows[pl.ds(k, 1)] = down[None]
    ends[0, pl.ds(pl.multiple_of(step * group, group), group), :] = x[:, 0, :]
    ends[1, pl.ds(pl.multiple_of(step * group, group), group), :] = x[:, m - 1, :]

    @pl.when(step == pl.num_programs(0) - 1)
    def _():
        line = Line(table[...], position, devices, m)
        one = line.power(1)
        up, down = up_rows[:, 0, :], down_rows[:, 7, :]
        for s in range(1, 8):
            up = up * one + up_rows[:, s, :]
            down = down * one + down_rows[:, 7 - s, :]
        first, last = ends[0], ends[1]
        lower, upper = line.corner * line.is_first * first, line.corner * line.is_last * last
        across = line.power(m - 1)
        up = line.rho * up + across * lower + upper
        down = line.rho * down + lower + across * upper
        going_up = line.green * (up - line.power(2 * line.near + m + 1) * down)
        going_down = line.green * (down - line.power(2 * line.far - m - 1) * up)
        for d in range(devices):
            ahead = d > position
            out[d, :planes, :] = jnp.where(ahead, going_up, going_down)
            out[d, planes:, :] = jnp.where(ahead, last, first)


def columns(theta, cut_far, cut_near, m):
    shape = (8, theta.shape[1])
    i = (lax.broadcasted_iota(jnp.int32, shape, 0) + (1 - m // 2)).astype(F32)
    down, up = jnp.exp(-theta * i), jnp.exp(theta * i)
    grow, fall = jnp.exp(theta * 8.0), jnp.exp(theta * -8.0)
    phi, chi = [], []
    for _ in range(m // 8):
        phi.append(down - cut_far * up)
        chi.append(up - cut_near * down)
        down, up = down * fall, up * grow
    return phi, chi


def local_kernel(dev_y, dev_z, rates_y, rates_z, x, out, sums, table, ytab, ztab, nz, band):
    step = pl.program_id(0)
    group, m, n = x.shape
    pos_y, pos_z = lax.axis_index("gy"), lax.axis_index("gz")

    @pl.when(step == 0)
    def _():
        spread(rates_y, table)
        y = Line(table[...], pos_y, dev_y, m)
        y.vectors()
        for i, row in enumerate(
            (y.theta, y.cut_far, y.cut_near, y.phi * y.weight, y.chi * y.weight, y.mid, y.side)
        ):
            ytab[i] = row
        spread(rates_z, table)
        z = Line(table[...], pos_z, dev_z, n)
        z.vectors()
        base = z.green * z.rho
        for i, row in enumerate(
            (z.theta, z.cut_far, z.cut_near, z.phi * base, z.chi * base, z.mid, z.side, z.corner / z.rho)
        ):
            ztab[i] = row
        for i, row in enumerate((z.send_up, z.send_down, z.head, z.tail)):
            nz[:, i, :] = row
            nz[:, 4 + i, :] = jnp.zeros_like(row)
        r = lax.broadcasted_iota(jnp.int32, (m, n), 0)
        c = lax.broadcasted_iota(jnp.int32, (m, n), 1)
        band[0] = jnp.where(r == c, 1.0, 0.0)
        band[1] = jnp.where((r == c + 1) | (r + 1 == c), 1.0, 0.0)

    z_first = jnp.where(pos_z == 0, 1.0, 0.0).astype(F32)
    z_last = jnp.where(pos_z == dev_z - 1, 1.0, 0.0).astype(F32)
    sub = lax.broadcasted_iota(jnp.int32, (8, n), 0)
    at_head = jnp.where(sub == 0, z_first, 0.0)
    at_tail = jnp.where(sub == 7, z_last, 0.0)

    def one(g, carry):
        k = step * group + g

        def rows(ref, i):
            return ref[i, pl.ds(k, 1), :]

        phi, chi = columns(rows(ytab, 0), rows(ytab, 1), rows(ytab, 2), m)
        phi_row, chi_row, mid, side = [rows(ytab, i) for i in (3, 4, 5, 6)]
        dmat = jnp.concatenate(
            [
                jnp.minimum(phi[v] * chi_row, chi[v] * phi_row)
                + mid * band[0, 8 * v : 8 * v + 8, :]
                + side * band[1, 8 * v : 8 * v + 8, :]
                for v in range(m // 8)
            ],
            axis=0,
        )
        d_hi, d_lo = split(dmat)
        x_hi, x_lo = split(x[g])
        turned = dot(
            jnp.concatenate([d_hi, d_lo, d_hi], axis=1),
            jnp.concatenate([x_hi, x_hi, x_lo], axis=0),
            1,
            0,
        )
        t_hi, t_lo = split(turned)

        phi, chi = columns(rows(ztab, 0), rows(ztab, 1), rows(ztab, 2), n)
        phi_row, chi_row, mid, side, edge = [rows(ztab, i) for i in (3, 4, 5, 6, 7)]
        head, tail = 1.0 + edge * at_head, 1.0 + edge * at_tail
        phi[0], chi[0] = phi[0] * head, chi[0] * head
        phi[-1], chi[-1] = phi[-1] * tail, chi[-1] * tail
        bmat = jnp.concatenate(
            [
                jnp.minimum(phi[v] * chi_row, chi[v] * phi_row)
                + mid * band[0, 8 * v : 8 * v + 8, :]
                + side * band[1, 8 * v : 8 * v + 8, :]
                for v in range(n // 8)
            ],
            axis=0,
        )
        b_hi, b_lo = split(bmat)
        out[g] = dot(
            jnp.concatenate([t_hi, t_lo, t_hi], axis=1),
            jnp.concatenate([b_hi, b_hi, b_lo], axis=0),
            1,
            0,
        )
        functionals = nz[pl.ds(k, 1)][0]
        f_hi = functionals.astype(BF16).astype(F32)
        f16 = jnp.concatenate([f_hi, functionals - f_hi], axis=0).astype(BF16)
        both = dot(f16, t_hi, 1, 1) + dot(f16, t_lo, 1, 1)
        sums[g] = both[:8] + both[8:]
        return carry

    lax.fori_loop(0, group, one, 0)


def along_lanes(line, f):
    m = line.m
    cell = line.cell
    near = 1.0 - line.power(2 * line.near) * jnp.exp(-2.0 * line.theta * (cell + 1).astype(F32))
    far = 1.0 - line.power(2 * (line.far - m - 1)) * jnp.exp(
        -2.0 * line.theta * (m - cell).astype(F32)
    )
    ups, downs = [], []
    span = 1
    while span < m:
        ratio = line.power(span)
        ups.append((span, jnp.where(cell >= span, ratio, 0.0)))
        downs.append((m - span, jnp.where(cell < m - span, ratio, 0.0)))
        span *= 2
    results = []
    for v in f:
        source = line.weight * v
        up, start = near * source, far * source
        for shift, ratio in ups:
            up = up + ratio * pltpu.roll(up, shift, 1)
        down = start
        for shift, ratio in downs:
            down = down + ratio * pltpu.roll(down, shift, 1)
        down = down - start
        left, right = pltpu.roll(v, 1, 1), pltpu.roll(v, m - 1, 1)
        left = jnp.where(cell > 0, left, 0.0)
        right = jnp.where(cell < m - 1, right, 0.0)
        results.append(far * up + near * down + line.mid * v + line.side * (left + right))
    return results


def incoming(ref, position, devices, reach, pick):
    up = jnp.zeros_like(reach)
    down = jnp.zeros_like(reach)
    for d in range(devices):
        up = jnp.where(d < position, up * reach + pick(d, 0), up)
        e = devices - 1 - d
        down = jnp.where(e > position, down * reach + pick(e, 1), down)
    return up, down


def middle_kernel(dev_y, dev_z, rates_y, rates_z, got, sums, send, held, table):
    planes, n = table.shape
    m = sums.shape[2]
    pos_y, pos_z = lax.axis_index("gy"), lax.axis_index("gz")
    spread(rates_y, table)
    y = Line(table[...], pos_y, dev_y, m)
    y.vectors()
    up, down = incoming(got, pos_y, dev_y, y.power(m), lambda d, kind: got[d, :planes, :])
    before = got[pl.ds(jnp.maximum(pos_y - 1, 0), 1), pl.ds(planes, planes), :][0]
    after = got[pl.ds(jnp.minimum(pos_y + 1, dev_y - 1), 1), pl.ds(planes, planes), :][0]
    before = jnp.where(pos_y > 0, before, 0.0)
    after = jnp.where(pos_y < dev_y - 1, after, 0.0)
    spread(rates_z, table)
    z = Line(table[...], pos_z, dev_z, n)
    z.vectors()
    arrivals = (up, down, before, after)
    places = (y.get_up, y.get_down, y.side * y.head, y.side * y.tail)
    for kind, functional in enumerate((z.send_up, z.send_down, z.head, z.tail)):
        total = sums[:, kind, :]
        for place, arrival in zip(places, arrivals):
            total = total + place * jnp.sum(arrival * functional, axis=1, keepdims=True)
        send[kind] = total
    for i, row in enumerate(along_lanes(z, arrivals)):
        held[i] = row


def final_kernel(dev_y, dev_z, rates_y, rates_z, local, held, got, out, table, left, right):
    step = pl.program_id(0)
    group, m, n = local.shape
    planes = table.shape[0]
    pos_y, pos_z = lax.axis_index("gy"), lax.axis_index("gz")

    @pl.when(step == 0)
    def _():
        spread(rates_y, table)
        y = Line(table[...], pos_y, dev_y, m)
        y.vectors()
        for i, row in enumerate((y.get_up, y.get_down, y.side * y.head, y.side * y.tail)):
            left[:, i, :] = row
            right[:, i, :] = held[i]
        spread(rates_z, table)
        z = Line(table[...], pos_z, dev_z, n)
        z.vectors()
        up, down = incoming(got, pos_z, dev_z, z.power(n), lambda d, kind: got[d, kind])
        before = got[pl.ds(jnp.maximum(pos_z - 1, 0), 1), 3][0]
        after = got[pl.ds(jnp.minimum(pos_z + 1, dev_z - 1), 1), 2][0]
        before = jnp.where(pos_z > 0, before, 0.0)
        after = jnp.where(pos_z < dev_z - 1, after, 0.0)
        for i, row in enumerate((up, down, before, after)):
            left[:, 4 + i, :] = row
        for i, row in enumerate((z.get_up, z.get_down, z.side * z.head, z.side * z.tail)):
            right[:, 4 + i, :] = row

    for g in range(group):
        k = step * group + g
        a, b = left[pl.ds(k, 1)][0], right[pl.ds(k, 1)][0]
        a_hi, b_hi = a.astype(BF16).astype(F32), b.astype(BF16).astype(F32)
        a_lo, b_lo = a - a_hi, b - b_hi
        a = jnp.concatenate([a_hi, a_lo, a_hi, a_lo], axis=0).astype(BF16)
        b = jnp.concatenate([b_hi, b_hi, b_lo, b_lo], axis=0).astype(BF16)
        out[g] = local[g] + dot(a, b, 0, 0)


def per_device(x, rates_y, rates_z):
    planes, m, n = x.shape
    dev_y, dev_z = lax.axis_size("gy"), lax.axis_size("gz")
    group = planes // STEPS
    smem = pl.BlockSpec(memory_space=pltpu.SMEM)
    whole = pl.BlockSpec(memory_space=pltpu.VMEM)
    slab = pl.BlockSpec((group, m, n), lambda i: (i, 0, 0))

    def params():
        return pltpu.CompilerParams(vmem_limit_bytes=VMEM)

    def cost(flops, moved):
        return pl.CostEstimate(flops=flops, bytes_accessed=moved, transcendentals=0)

    def shape(*dims):
        return jax.ShapeDtypeStruct(dims, F32)

    cells = planes * m * n
    payload = pl.pallas_call(
        functools.partial(moments_kernel, dev_y),
        grid=(STEPS,),
        in_specs=[smem, slab],
        out_specs=pl.BlockSpec((dev_y, 2 * planes, n), lambda i: (0, 0, 0)),
        out_shape=shape(dev_y, 2 * planes, n),
        scratch_shapes=[
            pltpu.VMEM((planes, n), F32),
            pltpu.VMEM((planes, n), F32),
            pltpu.VMEM((planes, 8, n), F32),
            pltpu.VMEM((planes, 8, n), F32),
            pltpu.VMEM((2, planes, n), F32),
        ],
        compiler_params=params(),
        cost_estimate=cost(4 * cells, 4 * cells),
        name="moments",
    )(rates_y, x)
    got_y = lax.all_to_all(payload, "gy", 0, 0, tiled=True)
    local, sums = pl.pallas_call(
        functools.partial(local_kernel, dev_y, dev_z),
        grid=(STEPS,),
        in_specs=[smem, smem, slab],
        out_specs=[slab, pl.BlockSpec((group, 8, m), lambda i: (i, 0, 0))],
        out_shape=[shape(planes, m, n), shape(planes, 8, m)],
        scratch_shapes=[
            pltpu.VMEM((planes, n), F32),
            pltpu.VMEM((7, planes, m), F32),
            pltpu.VMEM((8, planes, n), F32),
            pltpu.VMEM((planes, 8, n), F32),
            pltpu.VMEM((2, m, n), F32),
        ],
        compiler_params=params(),
        cost_estimate=cost(12 * cells * m, 8 * cells),
        name="local",
    )(rates_y, rates_z, x)
    send, held = pl.pallas_call(
        functools.partial(middle_kernel, dev_y, dev_z),
        in_specs=[smem, smem, whole, whole],
        out_specs=[whole, whole],
        out_shape=[shape(4, planes, m), shape(4, planes, n)],
        scratch_shapes=[pltpu.VMEM((planes, n), F32)],
        compiler_params=params(),
        cost_estimate=cost(planes * n * 400, planes * n * 100),
        name="middle",
    )(rates_y, rates_z, got_y, sums)
    got_z = lax.all_gather(send, "gz", axis=0, tiled=False)
    return pl.pallas_call(
        functools.partial(final_kernel, dev_y, dev_z),
        grid=(STEPS,),
        in_specs=[smem, smem, slab, whole, whole],
        out_specs=slab,
        out_shape=shape(planes, m, n),
        scratch_shapes=[
            pltpu.VMEM((planes, n), F32),
            pltpu.VMEM((planes, 8, m), F32),
            pltpu.VMEM((planes, 8, n), F32),
        ],
        compiler_params=params(),
        cost_estimate=cost(64 * cells, 8 * cells),
        name="final",
    )(rates_y, rates_z, local, held, got_z)


def solution(mesh):
    return jax.shard_map(
        per_device,
        mesh=mesh,
        in_specs=(P(None, "gy", "gz"), P(), P()),
        out_specs=P(None, "gy", "gz"),
        check_vma=False,
    )
```

profile of v0, /device:TPU:0, one launch (start us, length us, event | category | flops | bytes accessed | tf_op | source)
XLA Modules:
  0.0 37.7 jit_solution(6549565630055272562)
XLA Ops:
  0.0 0.0 copy-start
  0.0 1.6 %copy-done = f32[32,128,128]{2,1,0:T(8,128)S(1)} copy-done((f32[32,128,128]{2,1,0:T(8,128)S(1)}, f32[32,128,128]{2,1,0:T(8,128)}, u32[]{:S(2)}) %copy-start) | copy-done | bytes 2097176
  1.6 0.0 copy-start.4
  1.6 0.7 %copy-done.4 = f32[32]{0:T(128)S(1)} copy-done((f32[32]{0:T(128)S(1)}, f32[32]{0:T(128)}, u32[]{:S(2)}) %copy-start.4) | copy-done | bytes 152
  2.2 0.0 copy-start.1
  2.2 0.0 copy-start.5
  2.3 0.0 copy-start.6
  2.3 1.9 %moments.1 = f32[8,64,128]{2,1,0:T(8,128)} custom-call(f32[32]{0:T(128)S(1)} %copy-done.4, f32[32,128,128]{2,1,0:T(8,128)S(1)} %copy-done), custom_call_target="tpu_custom_call" | custom-call | flops 2097152 | bytes 2097152 | tf_op jit(solution)/shard_map/moments/pallas_call | solution.py:350
  4.2 7.3 %all-to-all-start = ((f32[8,64,128]{2,1,0:T(8,128)}), f32[8,64,128]{2,1,0:T(8,128)S(1)}, u32[]{:S(2)}, u32[]{:S(2)}) async-start(f32[8,64,128]{2,1,0:T(8,128)} %moments.1), calls=%async_computation | async-start | bytes 524288 | tf_op jit(solution)/shard_map/all_to_all | solution.py:367
  11.5 0.0 copy-done.1
  11.5 0.0 copy-done.5
  11.5 0.0 copy-done.6
  11.5 13.0 %local.1 = (f32[32,128,128]{2,1,0:T(8,128)S(1)}, f32[32,8,128]{2,1,0:T(8,128)S(1)}) custom-call(f32[32]{0:T(128)S(1)} %copy-done.5, f32[32]{0:T(128)S(1)} %copy-done.6, f32[32,128,128]{2,1,0:T(8,128)S(1)} %copy-done.1), custom_call_target="tpu_custom_call" | custom-call | flops 805306368 | bytes 4194304 | tf_op jit(solution)/shard_map/local/pallas_call | solution.py:368
  24.5 0.0 copy-start.2
  24.5 1.3 %copy-done.2 = f32[32,128,128]{2,1,0:T(8,128)} copy-done((f32[32,128,128]{2,1,0:T(8,128)}, f32[32,128,128]{2,1,0:T(8,128)S(1)}, u32[]{:S(2)}) %copy-start.2) | copy-done | bytes 2097176
  25.8 0.0 all-to-all-done.got
  25.8 1.3 %middle.1 = (f32[4,32,128]{2,1,0:T(8,128)S(1)}, f32[4,32,128]{2,1,0:T(8,128)S(1)}) custom-call(f32[32]{0:T(128)S(1)} %copy-done.5, f32[32]{0:T(128)S(1)} %copy-done.6, f32[8,64,128]{2,1,0:T(8,128)S(1)} %all-to-all-done.got, f32[32,8,128]{2,1,0:T(8,128)S(1)} %get-tuple-element.10.sums), custom_call_target="tpu_custom_call" | custom-call | flops 1638400 | bytes 409600 | tf_op jit(solution)/shard_map/middle/pallas_call | solution.py:385
  27.1 5.8 %all-gather = f32[16,32,128]{2,1,0:T(8,128)S(1)} all-gather(f32[4,32,128]{2,1,0:T(8,128)S(1)} %get-tuple-element.12), channel_id=2, replica_groups=mesh['gy'=8,'gz'=4] {'gz'}, dimensions={0}, use_global_device_ids=true | all-gather | bytes 327680 | tf_op jit(solution)/shard_map/all_gather | solution.py:395
  32.9 0.0 copy-start.3
  32.9 1.6 %copy-done.3 = f32[32,128,128]{2,1,0:T(8,128)S(1)} copy-done((f32[32,128,128]{2,1,0:T(8,128)S(1)}, f32[32,128,128]{2,1,0:T(8,128)}, u32[]{:S(2)}) %copy-start.3) | copy-done | bytes 2097176
  34.5 3.2 %final.1 = f32[32,128,128]{2,1,0:T(8,128)} custom-call(f32[32]{0:T(128)S(1)} %copy-done.5, f32[32]{0:T(128)S(1)} %copy-done.6, f32[32,128,128]{2,1,0:T(8,128)S(1)} %copy-done.3, f32[4,32,128]{2,1,0:T(8,128)S(1)} %get-tuple-element.11.held, f32[4,4,32,128]{3,2,1,0:T(8,128)S(1)} %bitcast.1), custom_call_target="tpu_custom_call" | custom-call | flops 33554432 | bytes 4194304 | tf_op jit(solution)/shard_map/final/pallas_call | solution.py:396
Async XLA Ops:
  0.0 1.6 %copy-start = (f32[32,128,128]{2,1,0:T(8,128)S(1)}, f32[32,128,128]{2,1,0:T(8,128)}, u32[]{:S(2)}) copy-start(f32[32,128,128]{2,1,0:T(8,128)} %x.3) | copy-start | bytes 6291460
  1.6 0.7 %copy-start.4 = (f32[32]{0:T(128)S(1)}, f32[32]{0:T(128)}, u32[]{:S(2)}) copy-start(f32[32]{0:T(128)} %rates_y.5) | copy-start | bytes 388
  2.2 9.2 %copy-start.1 = (f32[32,128,128]{2,1,0:T(8,128)S(1)}, f32[32,128,128]{2,1,0:T(8,128)}, u32[]{:S(2)}) copy-start(f32[32,128,128]{2,1,0:T(8,128)} %x.3) | copy-start | bytes 6291460
  2.2 9.2 %copy-start.5 = (f32[32]{0:T(128)S(1)}, f32[32]{0:T(128)}, u32[]{:S(2)}) copy-start(f32[32]{0:T(128)} %rates_y.5) | copy-start | bytes 388
  2.3 9.2 %copy-start.6 = (f32[32]{0:T(128)S(1)}, f32[32]{0:T(128)}, u32[]{:S(2)}) copy-start(f32[32]{0:T(128)} %rates_z.5) | copy-start | bytes 388
  4.2 21.6 %all-to-all-start = ((f32[8,64,128]{2,1,0:T(8,128)}), f32[8,64,128]{2,1,0:T(8,128)S(1)}, u32[]{:S(2)}, u32[]{:S(2)}) async-start(f32[8,64,128]{2,1,0:T(8,128)} %moments.1), calls=%async_computation | async-start | bytes 524288 | tf_op jit(solution)/shard_map/all_to_all | solution.py:367
  24.5 1.3 %copy-start.2 = (f32[32,128,128]{2,1,0:T(8,128)}, f32[32,128,128]{2,1,0:T(8,128)S(1)}, u32[]{:S(2)}) copy-start(f32[32,128,128]{2,1,0:T(8,128)S(1)} %get-tuple-element.9.local) | copy-start | bytes 6291460
  32.9 1.6 %copy-start.3 = (f32[32,128,128]{2,1,0:T(8,128)S(1)}, f32[32,128,128]{2,1,0:T(8,128)}, u32[]{:S(2)}) copy-start(f32[32,128,128]{2,1,0:T(8,128)} %copy-done.2) | copy-start | bytes 6291460
where the time goes:
time: 38 us; the launch traced here: 37.7 us
  Pallas kernels  19.4 us (51%)
  starting transfers between devices  7.28 us (19%)
  blocking collectives  5.79 us (15%)
  local copies, waits for them, and re-layouts  5.17 us (14%)
    pallas_call x1, Pallas kernels, per_device(): pl.pallas_call(functools.partial(local_kernel, dev_y, dev_z), grid=(STEPS...  13 us
    all_to_all x1, starting transfers between devices, per_device(): got_y = lax.all_to_all(payload, 'gy', 0, 0, tiled=True)  7.28 us
    all_gather x1, blocking collectives, per_device(): got_z = lax.all_gather(send, 'gz', axis=0, tiled=False)  5.79 us
    unnamed x14, local copies, waits for them, and re-layouts  5.17 us
    pallas_call x1, Pallas kernels, per_device(): pl.pallas_call(functools.partial(final_kernel, dev_y, dev_z), grid=(STEPS...  3.23 us
    pallas_call x1, Pallas kernels, per_device(): pl.pallas_call(functools.partial(moments_kernel, dev_y), grid=(STEPS,), i...  1.92 us
    pallas_call x1, Pallas kernels, per_device(): pl.pallas_call(functools.partial(middle_kernel, dev_y, dev_z), in_specs=[...  1.28 us
  transfers between devices with their start and end apart: 1, of which 0 were waited for; matrix products, arithmetic and copies ran while one was open for 0% of the time, Pallas kernels for 34%

commit v1 on v0

--- a/solution.py
+++ b/solution.py
@@ -14,6 +14,8 @@
 BF16 = jnp.bfloat16
 STEPS = 4
 VMEM = 24 * 1024 * 1024
+LOCALV = 24
+FINALV = 24
 
 
 def spread(rates, table):
@@ -73,49 +75,61 @@
     return lax.dot_general(a, b, (((ca,), (cb,)), ((), ())), preferred_element_type=F32)
 
 
-def moments_kernel(devices, rates, x, out, table, eighth, up_rows, down_rows, ends):
-    step = pl.program_id(0)
-    group, m = x.shape[0], x.shape[1]
-    planes = table.shape[0]
+def product(a_hi, a_lo, b_hi, b_lo):
+    b = jnp.concatenate([b_hi, b_lo], axis=1)
+    n = b_hi.shape[1]
+    both = dot(jnp.concatenate([a_hi, a_lo], axis=1), jnp.concatenate([b, b], axis=0), 1, 0)
+    return both[:, :n] + both[:, n:]
+
+
+def moments_kernel(
+    devices, rates_hbm, x_hbm, out, rates, x, rate_sem, x_sems, table, up_rows, down_rows
+):
+    planes, m, n = x.shape
+    parts = x_sems.shape[0]
+    group = planes // parts
     position = lax.axis_index("gy")
-
-    @pl.when(step == 0)
-    def _():
-        spread(rates, table)
-        eighth[...] = Line(table[...], position, devices, m).power(8)
-
-    for g in range(group):
-        k = step * group + g
-        ratio = jnp.broadcast_to(eighth[pl.ds(k, 1), :], (8, x.shape[2]))
-        up, down = x[g, 0:8, :], x[g, m - 8 : m, :]
-        for v in range(1, m // 8):
-            up = up * ratio + x[g, 8 * v : 8 * v + 8, :]
-            w = m - 8 - 8 * v
-            down = down * ratio + x[g, w : w + 8, :]
-        up_rows[pl.ds(k, 1)] = up[None]
-        down_rows[pl.ds(k, 1)] = down[None]
-    ends[0, pl.ds(pl.multiple_of(step * group, group), group), :] = x[:, 0, :]
-    ends[1, pl.ds(pl.multiple_of(step * group, group), group), :] = x[:, m - 1, :]
-
-    @pl.when(step == pl.num_programs(0) - 1)
-    def _():
-        line = Line(table[...], position, devices, m)
-        one = line.power(1)
-        up, down = up_rows[:, 0, :], down_rows[:, 7, :]
-        for s in range(1, 8):
-            up = up * one + up_rows[:, s, :]
-            down = down * one + down_rows[:, 7 - s, :]
-        first, last = ends[0], ends[1]
-        lower, upper = line.corner * line.is_first * first, line.corner * line.is_last * last
-        across = line.power(m - 1)
-        up = line.rho * up + across * lower + upper
-        down = line.rho * down + lower + across * upper
-        going_up = line.green * (up - line.power(2 * line.near + m + 1) * down)
-        going_down = line.green * (down - line.power(2 * line.far - m - 1) * up)
-        for d in range(devices):
-            ahead = d > position
-            out[d, :planes, :] = jnp.where(ahead, going_up, going_down)
-            out[d, planes:, :] = jnp.where(ahead, last, first)
+    rate_copy = pltpu.make_async_copy(rates_hbm, rates, rate_sem)
+    rate_copy.start()
+    copies = []
+    for i in range(parts):
+        some = pl.ds(i * group, group)
+        copies.append(pltpu.make_async_copy(x_hbm.at[some], x.at[some], x_sems.at[i]))
+        copies[i].start()
+    rate_copy.wait()
+    spread(rates, table)
+    line = Line(table[...], position, devices, m)
+    one = line.power(1)
+    eighth = line.power(8)
+    across = line.power(m - 1)
+    lower_scale, upper_scale = line.corner * line.is_first, line.corner * line.is_last
+    turn_up, turn_down = line.power(2 * line.near + m + 1), line.power(2 * line.far - m - 1)
+    table[...] = eighth
+    for i in range(parts):
+        copies[i].wait()
+        for k in range(i * group, i * group + group):
+            ratio = jnp.broadcast_to(table[k : k + 1, :], (8, n))
+            up, down = x[k, 0:8, :], x[k, m - 8 : m, :]
+            for v in range(1, m // 8):
+                up = up * ratio + x[k, 8 * v : 8 * v + 8, :]
+                w = m - 8 - 8 * v
+                down = down * ratio + x[k, w : w + 8, :]
+            up_rows[k] = up
+            down_rows[k] = down
+    up, down = up_rows[:, 0, :], down_rows[:, 7, :]
+    for s in range(1, 8):
+        up = up * one + up_rows[:, s, :]
+        down = down * one + down_rows[:, 7 - s, :]
+    first, last = x[:, 0, :], x[:, m - 1, :]
+    lower, upper = lower_scale * first, upper_scale * last
+    up = line.rho * up + across * lower + upper
+    down = line.rho * down + lower + across * upper
+    going_up = line.green * (up - turn_up * down)
+    going_down = line.green * (down - turn_down * up)
+    for d in range(devices):
+        ahead = d > position
+        out[d, :planes, :] = jnp.where(ahead, going_up, going_down)
+        out[d, planes:, :] = jnp.where(ahead, last, first)
 
 
 def columns(theta, cut_far, cut_near, m):
@@ -131,7 +145,9 @@
     return phi, chi
 
 
-def local_kernel(dev_y, dev_z, rates_y, rates_z, x, out, sums, table, ytab, ztab, nz, band):
+def local_kernel(
+    dev_y, dev_z, rates_y, rates_z, x, out, sums, ykeep, zkeep, table, ytab, ztab, nz, band
+):
     step = pl.program_id(0)
     group, m, n = x.shape
     pos_y, pos_z = lax.axis_index("gy"), lax.axis_index("gz")
@@ -145,6 +161,8 @@
             (y.theta, y.cut_far, y.cut_near, y.phi * y.weight, y.chi * y.weight, y.mid, y.side)
         ):
             ytab[i] = row
+        for i, row in enumerate((y.get_up, y.get_down, y.side * y.head, y.side * y.tail, y.power(m))):
+            ykeep[i] = row
         spread(rates_z, table)
         z = Line(table[...], pos_z, dev_z, n)
         z.vectors()
@@ -153,6 +171,10 @@
             (z.theta, z.cut_far, z.cut_near, z.phi * base, z.chi * base, z.mid, z.side, z.corner / z.rho)
         ):
             ztab[i] = row
+        for i, row in enumerate(
+            (z.get_up, z.get_down, z.side * z.head, z.side * z.tail, z.power(n), z.send_up, z.send_down)
+        ):
+            zkeep[i] = row
         for i, row in enumerate((z.send_up, z.send_down, z.head, z.tail)):
             nz[:, i, :] = row
             nz[:, 4 + i, :] = jnp.zeros_like(row)
@@ -186,12 +208,7 @@
         )
         d_hi, d_lo = split(dmat)
         x_hi, x_lo = split(x[g])
-        turned = dot(
-            jnp.concatenate([d_hi, d_lo, d_hi], axis=1),
-            jnp.concatenate([x_hi, x_hi, x_lo], axis=0),
-            1,
-            0,
-        )
+        turned = product(d_hi, d_lo, x_hi, x_lo)
         t_hi, t_lo = split(turned)
 
         phi, chi = columns(rows(ztab, 0), rows(ztab, 1), rows(ztab, 2), n)
@@ -209,20 +226,17 @@
             axis=0,
         )
         b_hi, b_lo = split(bmat)
-        out[g] = dot(
-            jnp.concatenate([t_hi, t_lo, t_hi], axis=1),
-            jnp.concatenate([b_hi, b_hi, b_lo], axis=0),
-            1,
-            0,
-        )
+        out[g] = product(t_hi, t_lo, b_hi, b_lo)
         functionals = nz[pl.ds(k, 1)][0]
         f_hi = functionals.astype(BF16).astype(F32)
         f16 = jnp.concatenate([f_hi, functionals - f_hi], axis=0).astype(BF16)
-        both = dot(f16, t_hi, 1, 1) + dot(f16, t_lo, 1, 1)
+        both = dot(
+            jnp.concatenate([f16, f16], axis=1), jnp.concatenate([t_hi, t_lo], axis=1), 1, 1
+        )
         sums[g] = both[:8] + both[8:]
         return carry
 
-    lax.fori_loop(0, group, one, 0)
+    lax.fori_loop(0, group, one, 0, unroll=True)
 
 
 def along_lanes(line, f):
@@ -266,67 +280,88 @@
     return up, down
 
 
-def middle_kernel(dev_y, dev_z, rates_y, rates_z, got, sums, send, held, table):
-    planes, n = table.shape
-    m = sums.shape[2]
-    pos_y, pos_z = lax.axis_index("gy"), lax.axis_index("gz")
-    spread(rates_y, table)
-    y = Line(table[...], pos_y, dev_y, m)
-    y.vectors()
-    up, down = incoming(got, pos_y, dev_y, y.power(m), lambda d, kind: got[d, :planes, :])
-    before = got[pl.ds(jnp.maximum(pos_y - 1, 0), 1), pl.ds(planes, planes), :][0]
-    after = got[pl.ds(jnp.minimum(pos_y + 1, dev_y - 1), 1), pl.ds(planes, planes), :][0]
-    before = jnp.where(pos_y > 0, before, 0.0)
-    after = jnp.where(pos_y < dev_y - 1, after, 0.0)
+def arrivals(dev_y, reach, got):
+    planes = reach.shape[0]
+    position = lax.axis_index("gy")
+    up, down = incoming(got, position, dev_y, reach, lambda d, kind: got[d, :planes, :])
+    before = got[pl.ds(jnp.maximum(position - 1, 0), 1), pl.ds(planes, planes), :][0]
+    after = got[pl.ds(jnp.minimum(position + 1, dev_y - 1), 1), pl.ds(planes, planes), :][0]
+    before = jnp.where(position > 0, before, 0.0)
+    after = jnp.where(position < dev_y - 1, after, 0.0)
+    return up, down, before, after
+
+
+def middle_kernel(dev_y, dev_z, got, sums, ykeep, zkeep, *sends):
+    pos_z = lax.axis_index("gz")
+    n = zkeep.shape[2]
+    rows = arrivals(dev_y, ykeep[4], got)
+    totals = []
+    for kind in range(4):
+        total = sums[:, kind, :]
+        for i, row in enumerate(rows):
+            if kind < 2:
+                amount = jnp.sum(row * zkeep[5 + kind], axis=1, keepdims=True)
+            else:
+                amount = row[:, :1] if kind == 2 else row[:, n - 1 :]
+            total = total + ykeep[i] * amount
+        totals.append(total)
+    up, down, head, tail = totals
+    for by, send in enumerate(sends):
+        ahead = pos_z + by + 1 < dev_z
+        send[0] = jnp.where(ahead, up, down)
+        send[1] = jnp.where(ahead, tail, head)
+
+
+def held_kernel(dev_y, dev_z, rates_z, got, ykeep, held, table):
     spread(rates_z, table)
-    z = Line(table[...], pos_z, dev_z, n)
+    z = Line(table[...], lax.axis_index("gz"), dev_z, table.shape[1])
     z.vectors()
-    arrivals = (up, down, before, after)
-    places = (y.get_up, y.get_down, y.side * y.head, y.side * y.tail)
-    for kind, functional in enumerate((z.send_up, z.send_down, z.head, z.tail)):
-        total = sums[:, kind, :]
-        for place, arrival in zip(places, arrivals):
-            total = total + place * jnp.sum(arrival * functional, axis=1, keepdims=True)
-        send[kind] = total
-    for i, row in enumerate(along_lanes(z, arrivals)):
+    for i, row in enumerate(along_lanes(z, arrivals(dev_y, ykeep[4], got))):
         held[i] = row
 
 
-def final_kernel(dev_y, dev_z, rates_y, rates_z, local, held, got, out, table, left, right):
-    step = pl.program_id(0)
-    group, m, n = local.shape
-    planes = table.shape[0]
-    pos_y, pos_z = lax.axis_index("gy"), lax.axis_index("gz")
-
-    @pl.when(step == 0)
-    def _():
-        spread(rates_y, table)
-        y = Line(table[...], pos_y, dev_y, m)
-        y.vectors()
-        for i, row in enumerate((y.get_up, y.get_down, y.side * y.head, y.side * y.tail)):
-            left[:, i, :] = row
-            right[:, i, :] = held[i]
-        spread(rates_z, table)
-        z = Line(table[...], pos_z, dev_z, n)
-        z.vectors()
-        up, down = incoming(got, pos_z, dev_z, z.power(n), lambda d, kind: got[d, kind])
-        before = got[pl.ds(jnp.maximum(pos_z - 1, 0), 1), 3][0]
-        after = got[pl.ds(jnp.minimum(pos_z + 1, dev_z - 1), 1), 2][0]
-        before = jnp.where(pos_z > 0, before, 0.0)
-        after = jnp.where(pos_z < dev_z - 1, after, 0.0)
-        for i, row in enumerate((up, down, before, after)):
-            left[:, 4 + i, :] = row
-        for i, row in enumerate((z.get_up, z.get_down, z.side * z.head, z.side * z.tail)):
-            right[:, 4 + i, :] = row
-
-    for g in range(group):
-        k = step * group + g
-        a, b = left[pl.ds(k, 1)][0], right[pl.ds(k, 1)][0]
-        a_hi, b_hi = a.astype(BF16).astype(F32), b.astype(BF16).astype(F32)
-        a_lo, b_lo = a - a_hi, b - b_hi
-        a = jnp.concatenate([a_hi, a_lo, a_hi, a_lo], axis=0).astype(BF16)
-        b = jnp.concatenate([b_hi, b_hi, b_lo, b_lo], axis=0).astype(BF16)
-        out[g] = local[g] + dot(a, b, 0, 0)
+def final_kernel(dev_z, local_hbm, held, ykeep, zkeep, *rest):
+    gots, rest = rest[: dev_z - 1], rest[dev_z - 1 :]
+    out_hbm, local, out, in_sems, out_sems, left, right = rest
+    planes, m, n = local.shape
+    parts = in_sems.shape[0]
+    group = planes // parts
+    pos_z = lax.axis_index("gz")
+    loads, stores = [], []
+    for i in range(parts):
+        some = pl.ds(i * group, group)
+        loads.append(pltpu.make_async_copy(local_hbm.at[some], local.at[some], in_sems.at[i]))
+        stores.append(pltpu.make_async_copy(out.at[some], out_hbm.at[some], out_sems.at[i]))
+        loads[i].start()
+    for i in range(4):
+        left[:, i, :] = ykeep[i]
+        right[:, i, :] = held[i]
+        right[:, 4 + i, :] = zkeep[i]
+    reach = zkeep[4]
+    up, down = jnp.zeros_like(gots[0][0]), jnp.zeros_like(gots[0][0])
+    scale = jnp.ones_like(reach)
+    for by in range(dev_z - 1):
+        up = up + jnp.where(pos_z > by, scale * gots[by][0], 0.0)
+        behind = gots[dev_z - 2 - by]
+        down = down + jnp.where(pos_z + by + 1 < dev_z, scale * behind[0], 0.0)
+        scale = scale * reach
+    left[:, 4, :] = up
+    left[:, 5, :] = down
+    left[:, 6, :] = jnp.where(pos_z > 0, gots[0][1], 0.0)
+    left[:, 7, :] = jnp.where(pos_z < dev_z - 1, gots[-1][1], 0.0)
+
+    for i in range(parts):
+        loads[i].wait()
+        for k in range(i * group, i * group + group):
+            a, b = left[k], right[k]
+            a_hi, b_hi = a.astype(BF16).astype(F32), b.astype(BF16).astype(F32)
+            a_lo, b_lo = a - a_hi, b - b_hi
+            a = jnp.concatenate([a_hi, a_lo, a_hi, a_lo], axis=0).astype(BF16)
+            b = jnp.concatenate([b_hi, b_hi, b_lo, b_lo], axis=0).astype(BF16)
+            out[k] = local[k] + dot(a, b, 0, 0)
+        stores[i].start()
+    for i in range(parts):
+        stores[i].wait()
 
 
 def per_device(x, rates_y, rates_z):
@@ -347,30 +382,45 @@
         return jax.ShapeDtypeStruct(dims, F32)
 
     cells = planes * m * n
+    hbm = pl.BlockSpec(memory_space=pltpu.HBM)
     payload = pl.pallas_call(
         functools.partial(moments_kernel, dev_y),
-        grid=(STEPS,),
-        in_specs=[smem, slab],
-        out_specs=pl.BlockSpec((dev_y, 2 * planes, n), lambda i: (0, 0, 0)),
+        in_specs=[hbm, hbm],
+        out_specs=whole,
         out_shape=shape(dev_y, 2 * planes, n),
         scratch_shapes=[
-            pltpu.VMEM((planes, n), F32),
+            pltpu.SMEM((planes,), F32),
+            pltpu.VMEM((planes, m, n), F32),
+            pltpu.SemaphoreType.DMA,
+            pltpu.SemaphoreType.DMA((8,)),
             pltpu.VMEM((planes, n), F32),
             pltpu.VMEM((planes, 8, n), F32),
             pltpu.VMEM((planes, 8, n), F32),
-            pltpu.VMEM((2, planes, n), F32),
         ],
-        compiler_params=params(),
+        compiler_params=pltpu.CompilerParams(vmem_limit_bytes=60 * 1024 * 1024),
         cost_estimate=cost(4 * cells, 4 * cells),
         name="moments",
     )(rates_y, x)
     got_y = lax.all_to_all(payload, "gy", 0, 0, tiled=True)
-    local, sums = pl.pallas_call(
+    def full(*dims):
+        return pl.BlockSpec(dims, lambda i: (0,) * len(dims))
+
+    local, sums, ykeep, zkeep = pl.pallas_call(
         functools.partial(local_kernel, dev_y, dev_z),
         grid=(STEPS,),
         in_specs=[smem, smem, slab],
-        out_specs=[slab, pl.BlockSpec((group, 8, m), lambda i: (i, 0, 0))],
-        out_shape=[shape(planes, m, n), shape(planes, 8, m)],
+        out_specs=[
+            slab,
+            pl.BlockSpec((group, 8, m), lambda i: (i, 0, 0)),
+            full(5, planes, m),
+            full(7, planes, n),
+        ],
+        out_shape=[
+            shape(planes, m, n),
+            shape(planes, 8, m),
+            shape(5, planes, m),
+            shape(7, planes, n),
+        ],
         scratch_shapes=[
             pltpu.VMEM((planes, n), F32),
             pltpu.VMEM((7, planes, m), F32),
@@ -378,36 +428,51 @@
             pltpu.VMEM((planes, 8, n), F32),
             pltpu.VMEM((2, m, n), F32),
         ],
-        compiler_params=params(),
+        compiler_params=pltpu.CompilerParams(vmem_limit_bytes=LOCALV * 1024 * 1024),
         cost_estimate=cost(12 * cells * m, 8 * cells),
         name="local",
     )(rates_y, rates_z, x)
-    send, held = pl.pallas_call(
+    sends = pl.pallas_call(
         functools.partial(middle_kernel, dev_y, dev_z),
-        in_specs=[smem, smem, whole, whole],
-        out_specs=[whole, whole],
-        out_shape=[shape(4, planes, m), shape(4, planes, n)],
+        in_specs=[whole] * 4,
+        out_specs=[whole] * (dev_z - 1),
+        out_shape=[shape(2, planes, m)] * (dev_z - 1),
+        compiler_params=params(),
+        cost_estimate=cost(planes * n * 100, planes * n * 100),
+        name="middle",
+    )(got_y, sums, ykeep, zkeep)
+    got_z = [
+        lax.ppermute(send, "gz", [(i, (i + by + 1) % dev_z) for i in range(dev_z)])
+        for by, send in enumerate(sends)
+    ]
+    held = pl.pallas_call(
+        functools.partial(held_kernel, dev_y, dev_z),
+        in_specs=[smem, whole, whole],
+        out_specs=whole,
+        out_shape=shape(4, planes, n),
         scratch_shapes=[pltpu.VMEM((planes, n), F32)],
         compiler_params=params(),
         cost_estimate=cost(planes * n * 400, planes * n * 100),
-        name="middle",
-    )(rates_y, rates_z, got_y, sums)
-    got_z = lax.all_gather(send, "gz", axis=0, tiled=False)
+        name="held",
+    )(rates_z, got_y, ykeep)
     return pl.pallas_call(
-        functools.partial(final_kernel, dev_y, dev_z),
-        grid=(STEPS,),
-        in_specs=[smem, smem, slab, whole, whole],
-        out_specs=slab,
+        functools.partial(final_kernel, dev_z),
+        in_specs=[hbm] + [whole] * (dev_z + 2),
+        out_specs=hbm,
         out_shape=shape(planes, m, n),
+        input_output_aliases={0: 0},
         scratch_shapes=[
-            pltpu.VMEM((planes, n), F32),
+            pltpu.VMEM((planes, m, n), F32),
+            pltpu.VMEM((planes, m, n), F32),
+            pltpu.SemaphoreType.DMA((4,)),
+            pltpu.SemaphoreType.DMA((4,)),
             pltpu.VMEM((planes, 8, m), F32),
             pltpu.VMEM((planes, 8, n), F32),
         ],
-        compiler_params=params(),
+        compiler_params=pltpu.CompilerParams(vmem_limit_bytes=FINALV * 1024 * 1024),
         cost_estimate=cost(64 * cells, 8 * cells),
         name="final",
-    )(rates_y, rates_z, local, held, got_z)
+    )(local, held, ykeep, zkeep, *got_z)
 
 
 def solution(mesh):

time: 38 us -> 27.2 us (0.72)
  blocking collectives: 5.79 us -> 0 us
  local copies, waits for them, and re-layouts: 5.17 us -> 0.01 us
  Pallas kernels: 19.4 us -> 14.5 us
  starting transfers between devices: 7.28 us -> 10.3 us
  waiting for transfers between devices: 0.01 us -> 1.9 us
    all_gather x1 -> x0, blocking collectives: 5.79 us -> none  [per_device(): got_z = lax.all_gather(send, 'gz', axis=0, tiled=False)]
    pallas_call x1, Pallas kernels: 13 us -> 7.39 us  [per_device(): pl.pallas_call(functools.partial(local_kernel, dev_y, dev_z), grid=(STEPS...]
    unnamed x14 -> x6, local copies, waits for them, and re-layouts: 5.17 us -> 0.01 us
    ppermute x0 -> x3, starting transfers between devices: none -> 3 us  [per_device(): lax.ppermute(send, 'gz', [(i, (i + by + 1) % dev_z) for i in range(dev_z)])]
    pallas_call x2 -> x3, Pallas kernels: 5.15 us -> 6.9 us  [the longest x1 2.96 us: per_device(): pl.pallas_call(functools.partial(final_kernel, dev_z), in_specs=[hbm] + [...]
    all_to_all x1, waiting for transfers between devices: 0.01 us -> 1.5 us  [per_device(): got_y = lax.all_to_all(payload, 'gy', 0, 0, tiled=True)]
    pallas_call x1, Pallas kernels: 1.28 us -> 0.18 us  [per_device(): pl.pallas_call(functools.partial(middle_kernel, dev_y, dev_z), in_specs=[...]
    ppermute x0 -> x3, waiting for transfers between devices: none -> 0.4 us  [per_device(): lax.ppermute(send, 'gz', [(i, (i + by + 1) % dev_z) for i in range(dev_z)])]
  transfers between devices with their start and end apart: 1 -> 4, of which waited for: 0 -> 2; matrix products, arithmetic and copies ran while one was open for 0% -> 0% of each run, Pallas kernels for 34% -> 32%
where the time goes in v1:
time: 27.2 us; the launch traced here: 26.8 us
  Pallas kernels  14.5 us (53%)
  starting transfers between devices  10.3 us (38%)
  waiting for transfers between devices  1.9 us (7%)
    pallas_call x1, Pallas kernels, per_device(): pl.pallas_call(functools.partial(local_kernel, dev_y, dev_z), grid=(STEPS...  7.39 us
    all_to_all x1, starting transfers between devices, per_device(): got_y = lax.all_to_all(payload, 'gy', 0, 0, tiled=True)  7.3 us
    ppermute x3, starting transfers between devices, per_device(): lax.ppermute(send, 'gz', [(i, (i + by + 1) % dev_z) for i in range(dev_z)])  3 us
    pallas_call x1, Pallas kernels, per_device(): pl.pallas_call(functools.partial(final_kernel, dev_z), in_specs=[hbm] + [...  2.96 us
    pallas_call x1, Pallas kernels, per_device(): pl.pallas_call(functools.partial(moments_kernel, dev_y), in_specs=[hbm, h...  2.76 us
    all_to_all x1, waiting for transfers between devices, per_device(): got_y = lax.all_to_all(payload, 'gy', 0, 0, tiled=True)  1.5 us
    pallas_call x1, Pallas kernels, per_device(): pl.pallas_call(functools.partial(held_kernel, dev_y, dev_z), in_specs=[sm...  1.17 us
  transfers between devices with their start and end apart: 4, of which 2 were waited for; matrix products, arithmetic and copies ran while one was open for 0% of the time, Pallas kernels for 32%

profile of v1, /device:TPU:0, one launch (start us, length us, event | category | flops | bytes accessed | tf_op | source)
XLA Modules:
  0.0 26.8 jit_solution(15571379140569492011)
XLA Ops:
  0.0 0.0 copy-start.1
  0.0 0.0 copy-start
  0.0 0.0 copy-start.2
  0.0 2.8 %moments.1 = f32[8,64,128]{2,1,0:T(8,128)} custom-call(f32[32]{0:T(128)} %rates_hbm.1, f32[32,128,128]{2,1,0:T(8,128)} %x_hbm.1), custom_call_target="tpu_custom_call" | custom-call | flops 2097152 | bytes 2097152 | tf_op jit(solution)/shard_map/moments/pallas_call | solution.py:386
  2.8 7.3 %all-to-all-start = ((f32[8,64,128]{2,1,0:T(8,128)}), f32[8,64,128]{2,1,0:T(8,128)S(1)}, u32[]{:S(2)}, u32[]{:S(2)}) async-start(f32[8,64,128]{2,1,0:T(8,128)} %moments.1), calls=%async_computation | async-start | bytes 524288 | tf_op jit(solution)/shard_map/all_to_all | solution.py:404
  10.1 0.0 copy-done.1
  10.1 0.0 copy-done
  10.1 0.0 copy-done.2
  10.1 7.4 %local.1 = (f32[32,128,128]{2,1,0:T(8,128)}, f32[32,8,128]{2,1,0:T(8,128)S(1)}, f32[5,32,128]{2,1,0:T(8,128)S(1)}, f32[7,32,128]{2,1,0:T(8,128)S(1)}) custom-call(f32[32]{0:T(128)S(1)} %copy-done.1, f32[32]{0:T(128)S(1)} %copy-done.2, f32[32,128,128]{2,1,0:T(8,128)S(1)} %copy-done), custom_call_target="tpu_custom_call" | custom-call | flops 805306368 | bytes 4194304 | tf_op jit(solution)/shard_map/local/pallas_call | solution.py:408
  17.5 1.5 %all-to-all-done.got = f32[8,64,128]{2,1,0:T(8,128)S(1)} async-done(((f32[8,64,128]{2,1,0:T(8,128)}), f32[8,64,128]{2,1,0:T(8,128)S(1)}, u32[]{:S(2)}, u32[]{:S(2)}) %all-to-all-start) | async-done | bytes 262176 | tf_op jit(solution)/shard_map/all_to_all | solution.py:404
  19.0 0.2 middle.1
  19.2 0.1 collective-permute-start
  19.2 1.6 %collective-permute-start.1 = (f32[2,32,128]{2,1,0:T(8,128)S(1)}, f32[2,32,128]{2,1,0:T(8,128)S(1)}, u32[]{:S(2)}, u32[]{:S(2)}) collective-permute-start(f32[2,32,128]{2,1,0:T(8,128)S(1)} %get-tuple-element.17), channel_id=1, source_target_pairs={{0,2},{1,3},{2,0},{3,1},{4,6},{5,7},{6,4},{7,5},{8,10},{9,11},{10,... | collective-permute-start | bytes 98312 | tf_op jit(solution)/shard_map/ppermute | solution.py:445
  20.8 1.4 %collective-permute-start.2 = (f32[2,32,128]{2,1,0:T(8,128)S(1)}, f32[2,32,128]{2,1,0:T(8,128)S(1)}, u32[]{:S(2)}, u32[]{:S(2)}) collective-permute-start(f32[2,32,128]{2,1,0:T(8,128)S(1)} %get-tuple-element.18), channel_id=1, source_target_pairs={{0,3},{1,0},{2,1},{3,2},{4,7},{5,4},{6,5},{7,6},{8,11},{9,8},{10,9... | collective-permute-start | bytes 98312 | tf_op jit(solution)/shard_map/ppermute | solution.py:445
  22.2 1.2 %held.1 = f32[4,32,128]{2,1,0:T(8,128)S(1)} custom-call(f32[32]{0:T(128)S(1)} %copy-done.2, f32[8,64,128]{2,1,0:T(8,128)S(1)} %all-to-all-done.got, f32[5,32,128]{2,1,0:T(8,128)S(1)} %get-tuple-element.13.ykeep), custom_call_target="tpu_custom_call" | custom-call | flops 1638400 | bytes 409600 | tf_op jit(solution)/shard_map/held/pallas_call | solution.py:448
  23.4 0.0 collective-permute-done.rest_0_
  23.4 0.0 collective-permute-done.1.rest_1_
  23.4 0.4 %collective-permute-done.2.rest_2_ = f32[2,32,128]{2,1,0:T(8,128)S(1)} collective-permute-done((f32[2,32,128]{2,1,0:T(8,128)S(1)}, f32[2,32,128]{2,1,0:T(8,128)S(1)}, u32[]{:S(2)}, u32[]{:S(2)}) %collective-permute-start.2) | collective-permute-done | bytes 32800 | tf_op jit(solution)/shard_map/ppermute | solution.py:445
  23.8 3.0 %final.1 = f32[32,128,128]{2,1,0:T(8,128)} custom-call(f32[32,128,128]{2,1,0:T(8,128)} %get-tuple-element.12.local_hbm, f32[4,32,128]{2,1,0:T(8,128)S(1)} %held.1, f32[5,32,128]{2,1,0:T(8,128)S(1)} %get-tuple-element.13.ykeep, f32[7,32,128]{2,1,0:T(8,128)S(1)} %get-tuple-element.14.zkeep, ...), custom_call_target="tpu_custom_call", output_to_operand_aliasing={{}: (0, {})} | custom-call | flops 33554432 | bytes 4194304 | tf_op jit(solution)/shard_map/final/pallas_call | solution.py:458
Async XLA Ops:
  0.0 10.1 %copy-start.1 = (f32[32]{0:T(128)S(1)}, f32[32]{0:T(128)}, u32[]{:S(2)}) copy-start(f32[32]{0:T(128)} %rates_hbm.1) | copy-start | bytes 388
  0.0 10.1 %copy-start = (f32[32,128,128]{2,1,0:T(8,128)S(1)}, f32[32,128,128]{2,1,0:T(8,128)}, u32[]{:S(2)}) copy-start(f32[32,128,128]{2,1,0:T(8,128)} %x_hbm.1) | copy-start | bytes 6291460
  0.0 10.1 %copy-start.2 = (f32[32]{0:T(128)S(1)}, f32[32]{0:T(128)}, u32[]{:S(2)}) copy-start(f32[32]{0:T(128)} %rates_z.3) | copy-start | bytes 388
  2.8 16.2 %all-to-all-start = ((f32[8,64,128]{2,1,0:T(8,128)}), f32[8,64,128]{2,1,0:T(8,128)S(1)}, u32[]{:S(2)}, u32[]{:S(2)}) async-start(f32[8,64,128]{2,1,0:T(8,128)} %moments.1), calls=%async_computation | async-start | bytes 524288 | tf_op jit(solution)/shard_map/all_to_all | solution.py:404
  19.2 4.2 %collective-permute-start = (f32[2,32,128]{2,1,0:T(8,128)S(1)}, f32[2,32,128]{2,1,0:T(8,128)S(1)}, u32[]{:S(2)}, u32[]{:S(2)}) collective-permute-start(f32[2,32,128]{2,1,0:T(8,128)S(1)} %get-tuple-element.16), channel_id=1, source_target_pairs={{0,1},{1,2},{2,3},{3,0},{4,5},{5,6},{6,7},{7,4},{8,9},{9,10},{10,1... | collective-permute-start | bytes 98312 | tf_op jit(solution)/shard_map/ppermute | solution.py:445
  19.2 4.1 %collective-permute-start.1 = (f32[2,32,128]{2,1,0:T(8,128)S(1)}, f32[2,32,128]{2,1,0:T(8,128)S(1)}, u32[]{:S(2)}, u32[]{:S(2)}) collective-permute-start(f32[2,32,128]{2,1,0:T(8,128)S(1)} %get-tuple-element.17), channel_id=1, source_target_pairs={{0,2},{1,3},{2,0},{3,1},{4,6},{5,7},{6,4},{7,5},{8,10},{9,11},{10,... | collective-permute-start | bytes 98312 | tf_op jit(solution)/shard_map/ppermute | solution.py:445
  20.8 3.0 %collective-permute-start.2 = (f32[2,32,128]{2,1,0:T(8,128)S(1)}, f32[2,32,128]{2,1,0:T(8,128)S(1)}, u32[]{:S(2)}, u32[]{:S(2)}) collective-permute-start(f32[2,32,128]{2,1,0:T(8,128)S(1)} %get-tuple-element.18), channel_id=1, source_target_pairs={{0,3},{1,0},{2,1},{3,2},{4,7},{5,4},{6,5},{7,6},{8,11},{9,8},{10,9... | collective-permute-start | bytes 98312 | tf_op jit(solution)/shard_map/ppermute | solution.py:445

commit v2 on v1

--- a/solution.py
+++ b/solution.py
@@ -12,10 +12,8 @@
 outer_weight = 3.0 / 44.0
 F32 = jnp.float32
 BF16 = jnp.bfloat16
-STEPS = 4
 VMEM = 24 * 1024 * 1024
-LOCALV = 24
-FINALV = 24
+MOMV = 60
 
 
 def spread(rates, table):
@@ -126,10 +124,10 @@
     down = line.rho * down + lower + across * upper
     going_up = line.green * (up - turn_up * down)
     going_down = line.green * (down - turn_down * up)
-    for d in range(devices):
-        ahead = d > position
-        out[d, :planes, :] = jnp.where(ahead, going_up, going_down)
-        out[d, planes:, :] = jnp.where(ahead, last, first)
+    out[0] = going_up
+    out[1] = going_down
+    out[2] = first
+    out[3] = last
 
 
 def columns(theta, cut_far, cut_near, m):
@@ -145,55 +143,60 @@
     return phi, chi
 
 
-def local_kernel(
-    dev_y, dev_z, rates_y, rates_z, x, out, sums, ykeep, zkeep, table, ytab, ztab, nz, band
-):
-    step = pl.program_id(0)
-    group, m, n = x.shape
+def make_tables(dev_y, dev_z, rates_y, rates_z, m, n, ykeep, zkeep, ytab, ztab, nz, table):
     pos_y, pos_z = lax.axis_index("gy"), lax.axis_index("gz")
-
-    @pl.when(step == 0)
-    def _():
-        spread(rates_y, table)
-        y = Line(table[...], pos_y, dev_y, m)
-        y.vectors()
-        for i, row in enumerate(
-            (y.theta, y.cut_far, y.cut_near, y.phi * y.weight, y.chi * y.weight, y.mid, y.side)
-        ):
-            ytab[i] = row
-        for i, row in enumerate((y.get_up, y.get_down, y.side * y.head, y.side * y.tail, y.power(m))):
-            ykeep[i] = row
-        spread(rates_z, table)
-        z = Line(table[...], pos_z, dev_z, n)
-        z.vectors()
-        base = z.green * z.rho
-        for i, row in enumerate(
-            (z.theta, z.cut_far, z.cut_near, z.phi * base, z.chi * base, z.mid, z.side, z.corner / z.rho)
-        ):
-            ztab[i] = row
-        for i, row in enumerate(
-            (z.get_up, z.get_down, z.side * z.head, z.side * z.tail, z.power(n), z.send_up, z.send_down)
-        ):
-            zkeep[i] = row
-        for i, row in enumerate((z.send_up, z.send_down, z.head, z.tail)):
-            nz[:, i, :] = row
-            nz[:, 4 + i, :] = jnp.zeros_like(row)
-        r = lax.broadcasted_iota(jnp.int32, (m, n), 0)
-        c = lax.broadcasted_iota(jnp.int32, (m, n), 1)
-        band[0] = jnp.where(r == c, 1.0, 0.0)
-        band[1] = jnp.where((r == c + 1) | (r + 1 == c), 1.0, 0.0)
-
+    spread(rates_y, table)
+    y = Line(table[...], pos_y, dev_y, m)
+    y.vectors()
+    for i, row in enumerate((y.get_up, y.get_down, y.side * y.head, y.side * y.tail, y.theta)):
+        ykeep[i] = row
+    for i, row in enumerate(
+        (y.theta, y.cut_far, y.cut_near, y.phi * y.weight, y.chi * y.weight, y.mid, y.side)
+    ):
+        ytab[i] = row
+    spread(rates_z, table)
+    z = Line(table[...], pos_z, dev_z, n)
+    z.vectors()
+    for i, row in enumerate(
+        (z.get_up, z.get_down, z.side * z.head, z.side * z.tail, z.power(n), z.send_up, z.send_down)
+    ):
+        zkeep[i] = row
+    base = z.green * z.rho
+    for i, row in enumerate(
+        (z.theta, z.cut_far, z.cut_near, z.phi * base, z.chi * base, z.mid, z.side, z.corner / z.rho)
+    ):
+        ztab[i] = row
+    for i, row in enumerate((z.send_up, z.send_down, z.head, z.tail)):
+        nz[:, i, :] = row
+        nz[:, 4 + i, :] = jnp.zeros_like(row)
+
+
+def local_kernel(dev_y, dev_z, lo, hi, *refs):
+    if lo == 0:
+        rates_y, rates_z, x, out, sums, ykeep, zkeep, ytab, ztab, nz, table = refs[:11]
+        make_tables(
+            dev_y, dev_z, rates_y, rates_z, x.shape[1], x.shape[2], ykeep, zkeep, ytab, ztab, nz, table
+        )
+    else:
+        x, ytab, ztab, nz, _, out, sums = refs[:7]
+    band = refs[-1]
+    m, n = x.shape[1:]
+    pos_z = lax.axis_index("gz")
+    r = lax.broadcasted_iota(jnp.int32, (m, n), 0)
+    c = lax.broadcasted_iota(jnp.int32, (m, n), 1)
+    band[0] = jnp.where(r == c, 1.0, 0.0)
+    band[1] = jnp.where((r == c + 1) | (r + 1 == c), 1.0, 0.0)
     z_first = jnp.where(pos_z == 0, 1.0, 0.0).astype(F32)
     z_last = jnp.where(pos_z == dev_z - 1, 1.0, 0.0).astype(F32)
     sub = lax.broadcasted_iota(jnp.int32, (8, n), 0)
     at_head = jnp.where(sub == 0, z_first, 0.0)
     at_tail = jnp.where(sub == 7, z_last, 0.0)
 
-    def one(g, carry):
-        k = step * group + g
+    for k in range(lo, hi):
+        g = k - lo
 
         def rows(ref, i):
-            return ref[i, pl.ds(k, 1), :]
+            return ref[i, k : k + 1, :]
 
         phi, chi = columns(rows(ytab, 0), rows(ytab, 1), rows(ytab, 2), m)
         phi_row, chi_row, mid, side = [rows(ytab, i) for i in (3, 4, 5, 6)]
@@ -207,7 +210,7 @@
             axis=0,
         )
         d_hi, d_lo = split(dmat)
-        x_hi, x_lo = split(x[g])
+        x_hi, x_lo = split(x[k])
         turned = product(d_hi, d_lo, x_hi, x_lo)
         t_hi, t_lo = split(turned)
 
@@ -227,16 +230,13 @@
         )
         b_hi, b_lo = split(bmat)
         out[g] = product(t_hi, t_lo, b_hi, b_lo)
-        functionals = nz[pl.ds(k, 1)][0]
+        functionals = nz[k]
         f_hi = functionals.astype(BF16).astype(F32)
         f16 = jnp.concatenate([f_hi, functionals - f_hi], axis=0).astype(BF16)
         both = dot(
             jnp.concatenate([f16, f16], axis=1), jnp.concatenate([t_hi, t_lo], axis=1), 1, 1
         )
         sums[g] = both[:8] + both[8:]
-        return carry
-
-    lax.fori_loop(0, group, one, 0, unroll=True)
 
 
 def along_lanes(line, f):
@@ -270,34 +270,66 @@
     return results
 
 
-def incoming(ref, position, devices, reach, pick):
-    up = jnp.zeros_like(reach)
-    down = jnp.zeros_like(reach)
-    for d in range(devices):
-        up = jnp.where(d < position, up * reach + pick(d, 0), up)
-        e = devices - 1 - d
-        down = jnp.where(e > position, down * reach + pick(e, 1), down)
-    return up, down
-
-
-def arrivals(dev_y, reach, got):
-    planes = reach.shape[0]
+def place_of(stage):
     position = lax.axis_index("gy")
-    up, down = incoming(got, position, dev_y, reach, lambda d, kind: got[d, :planes, :])
-    before = got[pl.ds(jnp.maximum(position - 1, 0), 1), pl.ds(planes, planes), :][0]
-    after = got[pl.ds(jnp.minimum(position + 1, dev_y - 1), 1), pl.ds(planes, planes), :][0]
-    before = jnp.where(position > 0, before, 0.0)
-    after = jnp.where(position < dev_y - 1, after, 0.0)
-    return up, down, before, after
-
-
-def middle_kernel(dev_y, dev_z, got, sums, ykeep, zkeep, *sends):
+    size = 1 << stage
+    return (position // size) % 2 == 1, position % size, size
+
+
+def receive(stage, theta, m, held_in, up_sum, down_sum, first, last):
+    upper, place, size = place_of(stage)
+    steps = jnp.where(upper, place, size - 1 - place).astype(F32)
+    scale = jnp.exp(-theta * (m * steps))
+    up, down, before, after = held_in
+    return (
+        jnp.where(upper, up + scale * up_sum, up),
+        jnp.where(upper, down, down + scale * down_sum),
+        jnp.where(upper & (place == 0), last, before),
+        jnp.where(jnp.logical_not(upper) & (place == size - 1), first, after),
+    )
+
+
+def combine_kernel(stage, last_stage, m, mine, got, *refs):
+    if stage:
+        held_in, ykeep, _, send, held_out = refs
+        before = [held_in[i] for i in range(4)]
+    else:
+        ykeep, _, send, held_out = refs
+        before = [jnp.zeros_like(mine[0])] * 4
+    theta = ykeep[4]
+    upper, _, size = place_of(stage)
+    for i, row in enumerate(receive(stage, theta, m, before, got[0], got[1], got[2], got[3])):
+        held_out[i] = row
+    far = jnp.exp(-theta * (m * size))
+    up = jnp.where(upper, mine[0] + far * got[0], got[0] + far * mine[0])
+    down = jnp.where(upper, got[1] + far * mine[1], mine[1] + far * got[1])
+    first = jnp.where(upper, got[2], mine[2])
+    last = jnp.where(upper, mine[3], got[3])
+    if stage + 1 < last_stage:
+        for i, row in enumerate((up, down, first, last)):
+            send[i] = row
+    else:
+        above, _, _ = place_of(last_stage)
+        send[0] = jnp.where(above, down, up)
+        send[1] = jnp.where(above, first, last)
+
+
+def arrivals(stage, m, ykeep, got, held_in):
+    before = [held_in[i] for i in range(4)]
+    return receive(stage, ykeep[4], m, before, got[0], got[0], got[1], got[1])
+
+
+def middle_kernel(stage, dev_z, bounds, got, held_in, ykeep, zkeep, *refs):
+    pieces, sends, sums = refs[: len(bounds) - 1], refs[len(bounds) - 1 : -1], refs[-1]
+    m = ykeep.shape[2]
     pos_z = lax.axis_index("gz")
     n = zkeep.shape[2]
-    rows = arrivals(dev_y, ykeep[4], got)
+    rows = arrivals(stage, m, ykeep, got, held_in)
     totals = []
     for kind in range(4):
-        total = sums[:, kind, :]
+        for piece, lo, hi in zip(pieces, bounds, bounds[1:]):
+            sums[kind, lo:hi, :] = piece[:, kind, :]
+        total = sums[kind]
         for i, row in enumerate(rows):
             if kind < 2:
                 amount = jnp.sum(row * zkeep[5 + kind], axis=1, keepdims=True)
@@ -312,27 +344,19 @@
         send[1] = jnp.where(ahead, tail, head)
 
 
-def held_kernel(dev_y, dev_z, rates_z, got, ykeep, held, table):
+def held_kernel(stage, dev_z, rates_z, got, held_in, ykeep, held, table):
     spread(rates_z, table)
     z = Line(table[...], lax.axis_index("gz"), dev_z, table.shape[1])
     z.vectors()
-    for i, row in enumerate(along_lanes(z, arrivals(dev_y, ykeep[4], got))):
+    for i, row in enumerate(along_lanes(z, arrivals(stage, ykeep.shape[2], ykeep, got, held_in))):
         held[i] = row
 
 
-def final_kernel(dev_z, local_hbm, held, ykeep, zkeep, *rest):
+def final_kernel(dev_z, bounds, held, ykeep, zkeep, *rest):
     gots, rest = rest[: dev_z - 1], rest[dev_z - 1 :]
-    out_hbm, local, out, in_sems, out_sems, left, right = rest
-    planes, m, n = local.shape
-    parts = in_sems.shape[0]
-    group = planes // parts
+    local, (out_hbm, out, out_sems, left, right) = rest[:-5], rest[-5:]
+    planes, m, n = out.shape
     pos_z = lax.axis_index("gz")
-    loads, stores = [], []
-    for i in range(parts):
-        some = pl.ds(i * group, group)
-        loads.append(pltpu.make_async_copy(local_hbm.at[some], local.at[some], in_sems.at[i]))
-        stores.append(pltpu.make_async_copy(out.at[some], out_hbm.at[some], out_sems.at[i]))
-        loads[i].start()
     for i in range(4):
         left[:, i, :] = ykeep[i]
         right[:, i, :] = held[i]
@@ -350,27 +374,30 @@
     left[:, 6, :] = jnp.where(pos_z > 0, gots[0][1], 0.0)
     left[:, 7, :] = jnp.where(pos_z < dev_z - 1, gots[-1][1], 0.0)
 
-    for i in range(parts):
-        loads[i].wait()
+    count = out_sems.shape[0]
+    group = planes // count
+    stores = []
+    for i in range(count):
         for k in range(i * group, i * group + group):
             a, b = left[k], right[k]
             a_hi, b_hi = a.astype(BF16).astype(F32), b.astype(BF16).astype(F32)
             a_lo, b_lo = a - a_hi, b - b_hi
             a = jnp.concatenate([a_hi, a_lo, a_hi, a_lo], axis=0).astype(BF16)
             b = jnp.concatenate([b_hi, b_hi, b_lo, b_lo], axis=0).astype(BF16)
-            out[k] = local[k] + dot(a, b, 0, 0)
+            piece = sum(k >= hi for hi in bounds[1:])
+            out[k] = local[piece][k - bounds[piece]] + dot(a, b, 0, 0)
+        some = pl.ds(i * group, group)
+        stores.append(pltpu.make_async_copy(out.at[some], out_hbm.at[some], out_sems.at[i]))
         stores[i].start()
-    for i in range(parts):
-        stores[i].wait()
+    for store in stores:
+        store.wait()
 
 
 def per_device(x, rates_y, rates_z):
     planes, m, n = x.shape
     dev_y, dev_z = lax.axis_size("gy"), lax.axis_size("gz")
-    group = planes // STEPS
     smem = pl.BlockSpec(memory_space=pltpu.SMEM)
     whole = pl.BlockSpec(memory_space=pltpu.VMEM)
-    slab = pl.BlockSpec((group, m, n), lambda i: (i, 0, 0))
 
     def params():
         return pltpu.CompilerParams(vmem_limit_bytes=VMEM)
@@ -383,11 +410,12 @@
 
     cells = planes * m * n
     hbm = pl.BlockSpec(memory_space=pltpu.HBM)
-    payload = pl.pallas_call(
+    hbm = pl.BlockSpec(memory_space=pltpu.HBM)
+    send = pl.pallas_call(
         functools.partial(moments_kernel, dev_y),
         in_specs=[hbm, hbm],
         out_specs=whole,
-        out_shape=shape(dev_y, 2 * planes, n),
+        out_shape=shape(4, planes, n),
         scratch_shapes=[
             pltpu.SMEM((planes,), F32),
             pltpu.VMEM((planes, m, n), F32),
@@ -397,82 +425,98 @@
             pltpu.VMEM((planes, 8, n), F32),
             pltpu.VMEM((planes, 8, n), F32),
         ],
-        compiler_params=pltpu.CompilerParams(vmem_limit_bytes=60 * 1024 * 1024),
+        compiler_params=pltpu.CompilerParams(vmem_limit_bytes=MOMV * 1024 * 1024),
         cost_estimate=cost(4 * cells, 4 * cells),
         name="moments",
     )(rates_y, x)
-    got_y = lax.all_to_all(payload, "gy", 0, 0, tiled=True)
-    def full(*dims):
-        return pl.BlockSpec(dims, lambda i: (0,) * len(dims))
-
-    local, sums, ykeep, zkeep = pl.pallas_call(
-        functools.partial(local_kernel, dev_y, dev_z),
-        grid=(STEPS,),
-        in_specs=[smem, smem, slab],
-        out_specs=[
-            slab,
-            pl.BlockSpec((group, 8, m), lambda i: (i, 0, 0)),
-            full(5, planes, m),
-            full(7, planes, n),
-        ],
-        out_shape=[
-            shape(planes, m, n),
-            shape(planes, 8, m),
-            shape(5, planes, m),
-            shape(7, planes, n),
-        ],
-        scratch_shapes=[
-            pltpu.VMEM((planes, n), F32),
-            pltpu.VMEM((7, planes, m), F32),
-            pltpu.VMEM((8, planes, n), F32),
-            pltpu.VMEM((planes, 8, n), F32),
-            pltpu.VMEM((2, m, n), F32),
-        ],
-        compiler_params=pltpu.CompilerParams(vmem_limit_bytes=LOCALV * 1024 * 1024),
-        cost_estimate=cost(12 * cells * m, 8 * cells),
-        name="local",
-    )(rates_y, rates_z, x)
+    stages = dev_y.bit_length() - 1
+    bounds = [planes * i // stages for i in range(stages + 1)]
+    parts, pieces = [], []
+    held_in = None
+    for stage in range(stages):
+        lo, hi = bounds[stage], bounds[stage + 1]
+        got = lax.ppermute(send, "gy", [(i, i ^ (1 << stage)) for i in range(dev_y)])
+        first = stage == 0
+        outs = [shape(hi - lo, m, n), shape(hi - lo, 8, m)]
+        if first:
+            given = (rates_y, rates_z, x)
+            in_specs = [smem, smem, whole]
+            outs += [
+                shape(5, planes, m),
+                shape(7, planes, n),
+                shape(7, planes, m),
+                shape(8, planes, n),
+                shape(planes, 8, n),
+            ]
+            scratch = [pltpu.VMEM((planes, n), F32)]
+        else:
+            given = (x, *tables, send)
+            in_specs = [whole] * 5
+            scratch = []
+        part, piece, *rest = pl.pallas_call(
+            functools.partial(local_kernel, dev_y, dev_z, lo, hi),
+            in_specs=in_specs,
+            out_specs=[whole] * len(outs),
+            out_shape=outs,
+            scratch_shapes=scratch
+            + [pltpu.VMEM((2, m, n), F32)],
+            compiler_params=params(),
+            cost_estimate=cost(12 * (hi - lo) * m * m * n, 8 * (hi - lo) * m * n),
+            name="local",
+        )(*given)
+        parts.append(part)
+        pieces.append(piece)
+        if first:
+            ykeep, zkeep, *tables = rest
+        if stage + 1 < stages:
+            send, held_in = pl.pallas_call(
+                functools.partial(combine_kernel, stage, stages - 1, m),
+                in_specs=[whole] * (4 if first else 5),
+                out_specs=[whole] * 2,
+                out_shape=[shape(4 if stage + 2 < stages else 2, planes, n), shape(4, planes, n)],
+                compiler_params=params(),
+                cost_estimate=cost(planes * n * 20, planes * n * 64),
+                name="combine",
+            )(send, got, *(() if first else (held_in,)), ykeep, piece)
     sends = pl.pallas_call(
-        functools.partial(middle_kernel, dev_y, dev_z),
-        in_specs=[whole] * 4,
+        functools.partial(middle_kernel, stages - 1, dev_z, bounds),
+        in_specs=[whole] * (4 + stages),
         out_specs=[whole] * (dev_z - 1),
         out_shape=[shape(2, planes, m)] * (dev_z - 1),
+        scratch_shapes=[pltpu.VMEM((4, planes, m), F32)],
         compiler_params=params(),
         cost_estimate=cost(planes * n * 100, planes * n * 100),
         name="middle",
-    )(got_y, sums, ykeep, zkeep)
+    )(got, held_in, ykeep, zkeep, *pieces)
     got_z = [
         lax.ppermute(send, "gz", [(i, (i + by + 1) % dev_z) for i in range(dev_z)])
         for by, send in enumerate(sends)
     ]
     held = pl.pallas_call(
-        functools.partial(held_kernel, dev_y, dev_z),
-        in_specs=[smem, whole, whole],
+        functools.partial(held_kernel, stages - 1, dev_z),
+        in_specs=[smem, whole, whole, whole],
         out_specs=whole,
         out_shape=shape(4, planes, n),
         scratch_shapes=[pltpu.VMEM((planes, n), F32)],
         compiler_params=params(),
         cost_estimate=cost(planes * n * 400, planes * n * 100),
         name="held",
-    )(rates_z, got_y, ykeep)
+    )(rates_z, got, held_in, ykeep)
     return pl.pallas_call(
-        functools.partial(final_kernel, dev_z),
-        in_specs=[hbm] + [whole] * (dev_z + 2),
+        functools.partial(final_kernel, dev_z, bounds),
+        in_specs=[whole] * (dev_z + 2 + stages),
         out_specs=hbm,
         out_shape=shape(planes, m, n),
-        input_output_aliases={0: 0},
         scratch_shapes=[
             pltpu.VMEM((planes, m, n), F32),
-            pltpu.VMEM((planes, m, n), F32),
-            pltpu.SemaphoreType.DMA((4,)),
             pltpu.SemaphoreType.DMA((4,)),
             pltpu.VMEM((planes, 8, m), F32),
             pltpu.VMEM((planes, 8, n), F32),
         ],
-        compiler_params=pltpu.CompilerParams(vmem_limit_bytes=FINALV * 1024 * 1024),
+        compiler_params=params(),
         cost_estimate=cost(64 * cells, 8 * cells),
         name="final",
-    )(local, held, ykeep, zkeep, *got_z)
+    )(held, ykeep, zkeep, *got_z, *parts)
 
 
 def solution(mesh):

time: 27.2 us -> 24.5 us (0.901)
  Pallas kernels: 14.5 us -> 11.8 us
  starting transfers between devices: 10.3 us -> 11.6 us
  waiting for transfers between devices: 1.9 us -> 0.81 us
    ppermute x0 -> x3, starting transfers between devices: none -> 8.28 us  [per_device(): got = lax.ppermute(send, 'gy', [(i, i ^ 1 << stage) for i in range(dev_y)])]
    all_to_all x1 -> x0, starting transfers between devices: 7.3 us -> none  [per_device(): got_y = lax.all_to_all(payload, 'gy', 0, 0, tiled=True)]
    pallas_call x4 -> x8, Pallas kernels: 11.7 us -> 9.23 us  [the longest x3 6.18 us: per_device(): pl.pallas_call(functools.partial(local_kernel, dev_y, dev_z, lo, hi), in_...]
    all_to_all x1 -> x0, waiting for transfers between devices: 1.5 us -> none  [per_device(): got_y = lax.all_to_all(payload, 'gy', 0, 0, tiled=True)]
    ppermute x0 -> x3, waiting for transfers between devices: none -> 0.39 us  [per_device(): got = lax.ppermute(send, 'gy', [(i, i ^ 1 << stage) for i in range(dev_y)])]
    ppermute x3, starting transfers between devices: 3 us -> 3.31 us  [per_device(): lax.ppermute(send, 'gz', [(i, (i + by + 1) % dev_z) for i in range(dev_z)])]
  transfers between devices with their start and end apart: 4 -> 6, of which waited for: 2 -> 2; matrix products, arithmetic and copies ran while one was open for 0% -> 0% of each run, Pallas kernels for 32% -> 30%
where the time goes in v2:
time: 24.5 us; the launch traced here: 24.3 us
  Pallas kernels  11.8 us (48%)
  starting transfers between devices  11.6 us (47%)
  waiting for transfers between devices  0.81 us (3%)
    ppermute x3, starting transfers between devices, per_device(): got = lax.ppermute(send, 'gy', [(i, i ^ 1 << stage) for i in range(dev_y)])  8.28 us
    pallas_call x3, Pallas kernels, per_device(): pl.pallas_call(functools.partial(local_kernel, dev_y, dev_z, lo, hi), in_...  6.18 us
    ppermute x3, starting transfers between devices, per_device(): lax.ppermute(send, 'gz', [(i, (i + by + 1) % dev_z) for i in range(dev_z)])  3.31 us
    pallas_call x1, Pallas kernels, per_device(): pl.pallas_call(functools.partial(moments_kernel, dev_y), in_specs=[hbm, h...  2.56 us
    pallas_call x1, Pallas kernels, per_device(): pl.pallas_call(functools.partial(final_kernel, dev_z, bounds), in_specs=[...  1.66 us
    pallas_call x1, Pallas kernels, per_device(): pl.pallas_call(functools.partial(held_kernel, stages - 1, dev_z), in_spec...  1.15 us
  transfers between devices with their start and end apart: 6, of which 2 were waited for; matrix products, arithmetic and copies ran while one was open for 0% of the time, Pallas kernels for 30%

profile of v2, /device:TPU:0, one launch (start us, length us, event | category | flops | bytes accessed | tf_op | source)
XLA Modules:
  0.0 24.3 jit_solution(12104252537128373789)
XLA Ops:
  0.0 0.0 copy-start
  0.0 0.0 copy-start.2
  0.0 0.0 copy-start.3
  0.0 2.6 %moments.1.mine = f32[4,32,128]{2,1,0:T(8,128)} custom-call(f32[32]{0:T(128)} %refs_0_.3, f32[32,128,128]{2,1,0:T(8,128)} %refs_0_.5), custom_call_target="tpu_custom_call" | custom-call | flops 2097152 | bytes 2097152 | tf_op jit(solution)/shard_map/moments/pallas_call | solution.py:414
  2.6 0.0 copy-start.1
  2.6 3.0 %collective-permute-start = (f32[4,32,128]{2,1,0:T(8,128)}, f32[4,32,128]{2,1,0:T(8,128)S(1)}, u32[]{:S(2)}, u32[]{:S(2)}) collective-permute-start(f32[4,32,128]{2,1,0:T(8,128)} %moments.1.mine), channel_id=1, source_target_pairs={{0,4},{4,0},{8,12},{12,8},{16,20},{20,16},{24,28},{28,24},{1,5},{5... | collective-permute-start | bytes 196616 | tf_op jit(solution)/shard_map/ppermute | solution.py:438
  5.6 0.0 copy-done
  5.6 0.0 copy-done.2
  5.6 0.0 copy-done.3
  5.6 2.4 %local.3 = (f32[10,128,128]{2,1,0:T(8,128)S(1)}, f32[10,8,128]{2,1,0:T(8,128)S(1)}, f32[5,32,128]{2,1,0:T(8,128)S(1)}, f32[7,32,128]{2,1,0:T(8,128)S(1)}, f32[7,...) custom-call(f32[32]{0:T(128)S(1)} %copy-done.2, f32[32]{0:T(128)S(1)} %copy-done.3, ...), custom_call_target="tpu_custom_call" | custom-call | flops 251658240 | bytes 1310720 | tf_op jit(solution)/shard_map/local/pallas_call | solution.py:456
  8.0 0.0 collective-permute-done.got
  8.1 0.0 copy-done.1
  8.1 2.1 %collective-permute-start.1 = (f32[4,32,128]{2,1,0:T(8,128)S(1)}, f32[4,32,128]{2,1,0:T(8,128)S(1)}, u32[]{:S(2)}, u32[]{:S(2)}) collective-permute-start(f32[4,32,128]{2,1,0:T(8,128)S(1)} %get-tuple-element.25.refs_4_.mine), channel_id=1, source_target_pairs={{0,8},{4,12},{8,0},{12,4},{16,24},{20,28},{24,16},{28,20},{1,9},{5... | collective-permute-start | bytes 196616 | tf_op jit(solution)/shard_map/ppermute | solution.py:438
  10.3 1.9 %local.4 = (f32[11,128,128]{2,1,0:T(8,128)S(1)}, f32[11,8,128]{2,1,0:T(8,128)S(1)}) custom-call(f32[32,128,128]{2,1,0:T(8,128)S(1)} %copy-done, f32[7,32,128]{2,1,0:T(8,128)S(1)} %get-tuple-element.27.refs_1_, f32[8,32,128]{2,1,0:T(8,128)S(1)} %get-tuple-element.28.refs_2_, f32[32,8,128]{2,1,0:T(8,128)S(1)} %get-tuple-element.29.refs_3_, ...), custom_call_target="tpu_custom_call" | custom-call | flops 276824064 | bytes 1441792 | tf_op jit(solution)/shard_map/local/pallas_call | solution.py:456
  12.2 0.3 %collective-permute-done.1.got = f32[4,32,128]{2,1,0:T(8,128)S(1)} collective-permute-done((f32[4,32,128]{2,1,0:T(8,128)S(1)}, f32[4,32,128]{2,1,0:T(8,128)S(1)}, u32[]{:S(2)}, u32[]{:S(2)}) %collective-permute-start.1) | collective-permute-done | bytes 65568 | tf_op jit(solution)/shard_map/ppermute | solution.py:438
  12.5 3.1 %collective-permute-start.2 = (f32[2,32,128]{2,1,0:T(8,128)S(1)}, f32[2,32,128]{2,1,0:T(8,128)S(1)}, u32[]{:S(2)}, u32[]{:S(2)}) collective-permute-start(f32[2,32,128]{2,1,0:T(8,128)S(1)} %get-tuple-element.31.refs_4_), channel_id=1, source_target_pairs={{0,16},{4,20},{8,24},{12,28},{16,0},{20,4},{24,8},{28,12},{1,17},{... | collective-permute-start | bytes 98312 | tf_op jit(solution)/shard_map/ppermute | solution.py:438
  15.6 1.9 %local.5 = (f32[11,128,128]{2,1,0:T(8,128)S(1)}, f32[11,8,128]{2,1,0:T(8,128)S(1)}) custom-call(f32[32,128,128]{2,1,0:T(8,128)S(1)} %copy-done, f32[7,32,128]{2,1,0:T(8,128)S(1)} %get-tuple-element.27.refs_1_, f32[8,32,128]{2,1,0:T(8,128)S(1)} %get-tuple-element.28.refs_2_, f32[32,8,128]{2,1,0:T(8,128)S(1)} %get-tuple-element.29.refs_3_, ...), custom_call_target="tpu_custom_call" | custom-call | flops 276824064 | bytes 1441792 | tf_op jit(solution)/shard_map/local/pallas_call | solution.py:456
  17.5 0.0 collective-permute-done.2.got
  17.5 0.2 middle.1
  17.7 0.1 collective-permute-start.3
  17.8 1.9 %collective-permute-start.4 = (f32[2,32,128]{2,1,0:T(8,128)S(1)}, f32[2,32,128]{2,1,0:T(8,128)S(1)}, u32[]{:S(2)}, u32[]{:S(2)}) collective-permute-start(f32[2,32,128]{2,1,0:T(8,128)S(1)} %get-tuple-element.36), channel_id=1, source_target_pairs={{0,2},{1,3},{2,0},{3,1},{4,6},{5,7},{6,4},{7,5},{8,10},{9,11},{10,... | collective-permute-start | bytes 98312 | tf_op jit(solution)/shard_map/ppermute | solution.py:492
  19.7 1.4 %collective-permute-start.5 = (f32[2,32,128]{2,1,0:T(8,128)S(1)}, f32[2,32,128]{2,1,0:T(8,128)S(1)}, u32[]{:S(2)}, u32[]{:S(2)}) collective-permute-start(f32[2,32,128]{2,1,0:T(8,128)S(1)} %get-tuple-element.37), channel_id=1, source_target_pairs={{0,3},{1,0},{2,1},{3,2},{4,7},{5,4},{6,5},{7,6},{8,11},{9,8},{10,9... | collective-permute-start | bytes 98312 | tf_op jit(solution)/shard_map/ppermute | solution.py:492
  21.1 1.2 %held.1 = f32[4,32,128]{2,1,0:T(8,128)S(1)} custom-call(f32[32]{0:T(128)S(1)} %copy-done.3, f32[2,32,128]{2,1,0:T(8,128)S(1)} %collective-permute-done.2.got, f32[4,32,128]{2,1,0:T(8,128)S(1)} %get-tuple-element.32.held_in, f32[5,32,128]{2,1,0:T(8,128)S(1)} %get-tuple-element.23.refs_0_.refs_1_.ykeep), custom_call_target="tpu_custom_call" | custom-call | flops 1638400 | bytes 409600 | tf_op jit(solution)/shard_map/held/pallas_call | solution.py:495
  22.2 0.0 collective-permute-done.3.rest_0_
  22.2 0.0 collective-permute-done.4.rest_1_
  22.2 0.4 %collective-permute-done.5.rest_2_ = f32[2,32,128]{2,1,0:T(8,128)S(1)} collective-permute-done((f32[2,32,128]{2,1,0:T(8,128)S(1)}, f32[2,32,128]{2,1,0:T(8,128)S(1)}, u32[]{:S(2)}, u32[]{:S(2)}) %collective-permute-start.5) | collective-permute-done | bytes 32800 | tf_op jit(solution)/shard_map/ppermute | solution.py:492
  22.7 1.7 %final.1 = f32[32,128,128]{2,1,0:T(8,128)} custom-call(f32[4,32,128]{2,1,0:T(8,128)S(1)} %held.1, f32[5,32,128]{2,1,0:T(8,128)S(1)} %get-tuple-element.23.refs_0_.refs_1_.ykeep, f32[7,32,128]{2,1,0:T(8,128)S(1)} %get-tuple-element.33.zkeep, f32[2,32,128]{2,1,0:T(8,128)S(1)} %collective-permute-done.3.rest_0_, ...), custom_call_target="tpu_custom_call" | custom-call | flops 33554432 | bytes 4194304 | tf_op jit(solution)/shard_map/final/pallas_call | solution.py:505
  (2 shorter events, 0.1 us)
Async XLA Ops:
  0.0 5.6 %copy-start = (f32[32,128,128]{2,1,0:T(8,128)S(1)}, f32[32,128,128]{2,1,0:T(8,128)}, u32[]{:S(2)}) copy-start(f32[32,128,128]{2,1,0:T(8,128)} %refs_0_.5) | copy-start | bytes 6291460
  0.0 5.6 %copy-start.2 = (f32[32]{0:T(128)S(1)}, f32[32]{0:T(128)}, u32[]{:S(2)}) copy-start(f32[32]{0:T(128)} %refs_0_.3) | copy-start | bytes 388
  0.0 5.6 %copy-start.3 = (f32[32]{0:T(128)S(1)}, f32[32]{0:T(128)}, u32[]{:S(2)}) copy-start(f32[32]{0:T(128)} %rates_z.1) | copy-start | bytes 388
  2.6 5.5 %copy-start.1 = (f32[4,32,128]{2,1,0:T(8,128)S(1)}, f32[4,32,128]{2,1,0:T(8,128)}, u32[]{:S(2)}) copy-start(f32[4,32,128]{2,1,0:T(8,128)} %moments.1.mine) | copy-start | bytes 196612
  2.6 5.5 %collective-permute-start = (f32[4,32,128]{2,1,0:T(8,128)}, f32[4,32,128]{2,1,0:T(8,128)S(1)}, u32[]{:S(2)}, u32[]{:S(2)}) collective-permute-start(f32[4,32,128]{2,1,0:T(8,128)} %moments.1.mine), channel_id=1, source_target_pairs={{0,4},{4,0},{8,12},{12,8},{16,20},{20,16},{24,28},{28,24},{1,5},{5... | collective-permute-start | bytes 196616 | tf_op jit(solution)/shard_map/ppermute | solution.py:438
  8.1 4.4 %collective-permute-start.1 = (f32[4,32,128]{2,1,0:T(8,128)S(1)}, f32[4,32,128]{2,1,0:T(8,128)S(1)}, u32[]{:S(2)}, u32[]{:S(2)}) collective-permute-start(f32[4,32,128]{2,1,0:T(8,128)S(1)} %get-tuple-element.25.refs_4_.mine), channel_id=1, source_target_pairs={{0,8},{4,12},{8,0},{12,4},{16,24},{20,28},{24,16},{28,20},{1,9},{5... | collective-permute-start | bytes 196616 | tf_op jit(solution)/shard_map/ppermute | solution.py:438
  12.5 5.0 %collective-permute-start.2 = (f32[2,32,128]{2,1,0:T(8,128)S(1)}, f32[2,32,128]{2,1,0:T(8,128)S(1)}, u32[]{:S(2)}, u32[]{:S(2)}) collective-permute-start(f32[2,32,128]{2,1,0:T(8,128)S(1)} %get-tuple-element.31.refs_4_), channel_id=1, source_target_pairs={{0,16},{4,20},{8,24},{12,28},{16,0},{20,4},{24,8},{28,12},{1,17},{... | collective-permute-start | bytes 98312 | tf_op jit(solution)/shard_map/ppermute | solution.py:438
  17.7 4.5 %collective-permute-start.3 = (f32[2,32,128]{2,1,0:T(8,128)S(1)}, f32[2,32,128]{2,1,0:T(8,128)S(1)}, u32[]{:S(2)}, u32[]{:S(2)}) collective-permute-start(f32[2,32,128]{2,1,0:T(8,128)S(1)} %get-tuple-element.35), channel_id=1, source_target_pairs={{0,1},{1,2},{2,3},{3,0},{4,5},{5,6},{6,7},{7,4},{8,9},{9,10},{10,1... | collective-permute-start | bytes 98312 | tf_op jit(solution)/shard_map/ppermute | solution.py:492
  17.8 4.4 %collective-permute-start.4 = (f32[2,32,128]{2,1,0:T(8,128)S(1)}, f32[2,32,128]{2,1,0:T(8,128)S(1)}, u32[]{:S(2)}, u32[]{:S(2)}) collective-permute-start(f32[2,32,128]{2,1,0:T(8,128)S(1)} %get-tuple-element.36), channel_id=1, source_target_pairs={{0,2},{1,3},{2,0},{3,1},{4,6},{5,7},{6,4},{7,5},{8,10},{9,11},{10,... | collective-permute-start | bytes 98312 | tf_op jit(solution)/shard_map/ppermute | solution.py:492
  19.7 3.0 %collective-permute-start.5 = (f32[2,32,128]{2,1,0:T(8,128)S(1)}, f32[2,32,128]{2,1,0:T(8,128)S(1)}, u32[]{:S(2)}, u32[]{:S(2)}) collective-permute-start(f32[2,32,128]{2,1,0:T(8,128)S(1)} %get-tuple-element.37), channel_id=1, source_target_pairs={{0,3},{1,0},{2,1},{3,2},{4,7},{5,4},{6,5},{7,6},{8,11},{9,8},{10,9... | collective-permute-start | bytes 98312 | tf_op jit(solution)/shard_map/ppermute | solution.py:492

commit v3 on v2

--- a/solution.py
+++ b/solution.py
@@ -13,7 +13,8 @@
 F32 = jnp.float32
 BF16 = jnp.bfloat16
 VMEM = 24 * 1024 * 1024
-MOMV = 60
+FETCH_VMEM = 50 * 1024 * 1024
+CUTS = (0, 2, 5, 10, 16)
 
 
 def spread(rates, table):
@@ -80,21 +81,21 @@
     return both[:, :n] + both[:, n:]
 
 
-def moments_kernel(
-    devices, rates_hbm, x_hbm, out, rates, x, rate_sem, x_sems, table, up_rows, down_rows
-):
-    planes, m, n = x.shape
-    parts = x_sems.shape[0]
-    group = planes // parts
-    position = lax.axis_index("gy")
-    rate_copy = pltpu.make_async_copy(rates_hbm, rates, rate_sem)
-    rate_copy.start()
+def fetch_kernel(x_hbm, x, sems):
+    parts = sems.shape[0]
+    group = x.shape[0] // parts
     copies = []
     for i in range(parts):
         some = pl.ds(i * group, group)
-        copies.append(pltpu.make_async_copy(x_hbm.at[some], x.at[some], x_sems.at[i]))
+        copies.append(pltpu.make_async_copy(x_hbm.at[some], x.at[some], sems.at[i]))
         copies[i].start()
-    rate_copy.wait()
+    for copy in copies:
+        copy.wait()
+
+
+def moments_kernel(devices, rates, x, out, table, up_rows, down_rows):
+    planes, m, n = x.shape
+    position = lax.axis_index("gy")
     spread(rates, table)
     line = Line(table[...], position, devices, m)
     one = line.power(1)
@@ -103,9 +104,8 @@
     lower_scale, upper_scale = line.corner * line.is_first, line.corner * line.is_last
     turn_up, turn_down = line.power(2 * line.near + m + 1), line.power(2 * line.far - m - 1)
     table[...] = eighth
-    for i in range(parts):
-        copies[i].wait()
-        for k in range(i * group, i * group + group):
+    if True:
+        for k in range(planes):
             ratio = jnp.broadcast_to(table[k : k + 1, :], (8, n))
             up, down = x[k, 0:8, :], x[k, m - 8 : m, :]
             for v in range(1, m // 8):
@@ -298,20 +298,28 @@
         before = [jnp.zeros_like(mine[0])] * 4
     theta = ykeep[4]
     upper, _, size = place_of(stage)
-    for i, row in enumerate(receive(stage, theta, m, before, got[0], got[1], got[2], got[3])):
-        held_out[i] = row
+    row, end = got.shape[0] - 1, got.shape[0] - 2 if stage == 0 else got.shape[0] - 1
+    lows = (got[0], got[1], got[end], got[row])
+    for i, value in enumerate(receive(stage, theta, m, before, *lows)):
+        held_out[i] = value
     far = jnp.exp(-theta * (m * size))
     up = jnp.where(upper, mine[0] + far * got[0], got[0] + far * mine[0])
     down = jnp.where(upper, got[1] + far * mine[1], mine[1] + far * got[1])
-    first = jnp.where(upper, got[2], mine[2])
-    last = jnp.where(upper, mine[3], got[3])
+    _, place, _ = place_of(stage + 1)
+    if stage == 0:
+        first = jnp.where(upper, got[2], mine[2])
+        last = jnp.where(upper, mine[3], got[3])
+        halo = jnp.where(place == 0, last, first)
+    else:
+        halo = got[2]
     if stage + 1 < last_stage:
-        for i, row in enumerate((up, down, first, last)):
-            send[i] = row
+        send[0] = up
+        send[1] = down
+        send[2] = halo
     else:
         above, _, _ = place_of(last_stage)
         send[0] = jnp.where(above, down, up)
-        send[1] = jnp.where(above, first, last)
+        send[1] = halo
 
 
 def arrivals(stage, m, ykeep, got, held_in):
@@ -344,23 +352,26 @@
         send[1] = jnp.where(ahead, tail, head)
 
 
-def held_kernel(stage, dev_z, rates_z, got, held_in, ykeep, held, table):
+def held_kernel(stage, dev_z, rates_z, got, held_in, ykeep, zkeep, right_split, table, right):
     spread(rates_z, table)
     z = Line(table[...], lax.axis_index("gz"), dev_z, table.shape[1])
     z.vectors()
     for i, row in enumerate(along_lanes(z, arrivals(stage, ykeep.shape[2], ykeep, got, held_in))):
-        held[i] = row
-
-
-def final_kernel(dev_z, bounds, held, ykeep, zkeep, *rest):
+        right[:, i, :] = row
+        right[:, 4 + i, :] = zkeep[i]
+    b = right[...]
+    hi = b.astype(BF16).astype(F32)
+    lo = b - hi
+    right_split[...] = jnp.concatenate([hi, hi, lo, lo], axis=1).astype(BF16)
+
+
+def final_kernel(dev_z, bounds, right, ykeep, zkeep, *rest):
     gots, rest = rest[: dev_z - 1], rest[dev_z - 1 :]
-    local, (out_hbm, out, out_sems, left, right) = rest[:-5], rest[-5:]
+    local, (out_hbm, out, out_sems, left) = rest[:-4], rest[-4:]
     planes, m, n = out.shape
     pos_z = lax.axis_index("gz")
     for i in range(4):
         left[:, i, :] = ykeep[i]
-        right[:, i, :] = held[i]
-        right[:, 4 + i, :] = zkeep[i]
     reach = zkeep[4]
     up, down = jnp.zeros_like(gots[0][0]), jnp.zeros_like(gots[0][0])
     scale = jnp.ones_like(reach)
@@ -374,19 +385,17 @@
     left[:, 6, :] = jnp.where(pos_z > 0, gots[0][1], 0.0)
     left[:, 7, :] = jnp.where(pos_z < dev_z - 1, gots[-1][1], 0.0)
 
-    count = out_sems.shape[0]
-    group = planes // count
+    cuts = [planes * c // 16 for c in CUTS]
     stores = []
-    for i in range(count):
-        for k in range(i * group, i * group + group):
-            a, b = left[k], right[k]
-            a_hi, b_hi = a.astype(BF16).astype(F32), b.astype(BF16).astype(F32)
-            a_lo, b_lo = a - a_hi, b - b_hi
+    for i, (lo, hi) in enumerate(zip(cuts, cuts[1:])):
+        for k in range(lo, hi):
+            a = left[k]
+            a_hi = a.astype(BF16).astype(F32)
+            a_lo = a - a_hi
             a = jnp.concatenate([a_hi, a_lo, a_hi, a_lo], axis=0).astype(BF16)
-            b = jnp.concatenate([b_hi, b_hi, b_lo, b_lo], axis=0).astype(BF16)
-            piece = sum(k >= hi for hi in bounds[1:])
-            out[k] = local[piece][k - bounds[piece]] + dot(a, b, 0, 0)
-        some = pl.ds(i * group, group)
+            piece = sum(k >= bound for bound in bounds[1:])
+            out[k] = local[piece][k - bounds[piece]] + dot(a, right[k], 0, 0)
+        some = pl.ds(lo, hi - lo)
         stores.append(pltpu.make_async_copy(out.at[some], out_hbm.at[some], out_sems.at[i]))
         stores[i].start()
     for store in stores:
@@ -411,21 +420,27 @@
     cells = planes * m * n
     hbm = pl.BlockSpec(memory_space=pltpu.HBM)
     hbm = pl.BlockSpec(memory_space=pltpu.HBM)
+    x = pl.pallas_call(
+        fetch_kernel,
+        in_specs=[hbm],
+        out_specs=whole,
+        out_shape=shape(planes, m, n),
+        scratch_shapes=[pltpu.SemaphoreType.DMA((8,))],
+        compiler_params=pltpu.CompilerParams(vmem_limit_bytes=FETCH_VMEM),
+        cost_estimate=cost(4, 8 * cells),
+        name="fetch",
+    )(x)
     send = pl.pallas_call(
         functools.partial(moments_kernel, dev_y),
-        in_specs=[hbm, hbm],
+        in_specs=[smem, whole],
         out_specs=whole,
         out_shape=shape(4, planes, n),
         scratch_shapes=[
-            pltpu.SMEM((planes,), F32),
-            pltpu.VMEM((planes, m, n), F32),
-            pltpu.SemaphoreType.DMA,
-            pltpu.SemaphoreType.DMA((8,)),
             pltpu.VMEM((planes, n), F32),
             pltpu.VMEM((planes, 8, n), F32),
             pltpu.VMEM((planes, 8, n), F32),
         ],
-        compiler_params=pltpu.CompilerParams(vmem_limit_bytes=MOMV * 1024 * 1024),
+        compiler_params=params(),
         cost_estimate=cost(4 * cells, 4 * cells),
         name="moments",
     )(rates_y, x)
@@ -473,7 +488,7 @@
                 functools.partial(combine_kernel, stage, stages - 1, m),
                 in_specs=[whole] * (4 if first else 5),
                 out_specs=[whole] * 2,
-                out_shape=[shape(4 if stage + 2 < stages else 2, planes, n), shape(4, planes, n)],
+                out_shape=[shape(3 if stage + 2 < stages else 2, planes, n), shape(4, planes, n)],
                 compiler_params=params(),
                 cost_estimate=cost(planes * n * 20, planes * n * 64),
                 name="combine",
@@ -494,14 +509,14 @@
     ]
     held = pl.pallas_call(
         functools.partial(held_kernel, stages - 1, dev_z),
-        in_specs=[smem, whole, whole, whole],
+        in_specs=[smem, whole, whole, whole, whole],
         out_specs=whole,
-        out_shape=shape(4, planes, n),
-        scratch_shapes=[pltpu.VMEM((planes, n), F32)],
+        out_shape=jax.ShapeDtypeStruct((planes, 32, n), BF16),
+        scratch_shapes=[pltpu.VMEM((planes, n), F32), pltpu.VMEM((planes, 8, n), F32)],
         compiler_params=params(),
         cost_estimate=cost(planes * n * 400, planes * n * 100),
         name="held",
-    )(rates_z, got, held_in, ykeep)
+    )(rates_z, got, held_in, ykeep, zkeep)
     return pl.pallas_call(
         functools.partial(final_kernel, dev_z, bounds),
         in_specs=[whole] * (dev_z + 2 + stages),
@@ -509,9 +524,8 @@
         out_shape=shape(planes, m, n),
         scratch_shapes=[
             pltpu.VMEM((planes, m, n), F32),
-            pltpu.SemaphoreType.DMA((4,)),
+            pltpu.SemaphoreType.DMA((len(CUTS) - 1,)),
             pltpu.VMEM((planes, 8, m), F32),
-            pltpu.VMEM((planes, 8, n), F32),
         ],
         compiler_params=params(),
         cost_estimate=cost(64 * cells, 8 * cells),

time: 24.5 us -> 24.1 us (0.984)
  starting transfers between devices: 11.6 us -> 11.3 us
    ppermute x3, starting transfers between devices: 8.28 us -> 7.98 us  [per_device(): got = lax.ppermute(send, 'gy', [(i, i ^ 1 << stage) for i in range(dev_y)])]
    pallas_call x1 -> x2, Pallas kernels: 2.56 us -> 2.67 us  [the longest x1 1.58 us: per_device(): pl.pallas_call(fetch_kernel, in_specs=[hbm], out_specs=whole, out_shape=s...]
  transfers between devices with their start and end apart: 6 -> 6, of which waited for: 2 -> 2; matrix products, arithmetic and copies ran while one was open for 0% -> 0% of each run, Pallas kernels for 30% -> 31%
where the time goes in v3:
time: 24.1 us; the launch traced here: 24 us
  Pallas kernels  11.9 us (49%)
  starting transfers between devices  11.3 us (47%)
  waiting for transfers between devices  0.63 us (3%)
    ppermute x3, starting transfers between devices, per_device(): got = lax.ppermute(send, 'gy', [(i, i ^ 1 << stage) for i in range(dev_y)])  7.98 us
    pallas_call x3, Pallas kernels, per_device(): pl.pallas_call(functools.partial(local_kernel, dev_y, dev_z, lo, hi), in_...  6.18 us
    ppermute x3, starting transfers between devices, per_device(): lax.ppermute(send, 'gz', [(i, (i + by + 1) % dev_z) for i in range(dev_z)])  3.31 us
    pallas_call x1, Pallas kernels, per_device(): pl.pallas_call(functools.partial(final_kernel, dev_z, bounds), in_specs=[...  1.61 us
    pallas_call x1, Pallas kernels, per_device(): pl.pallas_call(fetch_kernel, in_specs=[hbm], out_specs=whole, out_shape=s...  1.58 us
    pallas_call x1, Pallas kernels, per_device(): pl.pallas_call(functools.partial(held_kernel, stages - 1, dev_z), in_spec...  1.24 us
    pallas_call x1, Pallas kernels, per_device(): pl.pallas_call(functools.partial(moments_kernel, dev_y), in_specs=[smem,...  1.08 us
  transfers between devices with their start and end apart: 6, of which 2 were waited for; matrix products, arithmetic and copies ran while one was open for 0% of the time, Pallas kernels for 31%

profile of v3, /device:TPU:0, one launch (start us, length us, event | category | flops | bytes accessed | tf_op | source)
XLA Modules:
  0.0 24.0 jit_solution(5223522088030009601)
XLA Ops:
  0.0 0.0 copy-start
  0.0 1.6 %fetch.1.x.refs_2_.refs_0_ = f32[32,128,128]{2,1,0:T(8,128)S(1)} custom-call(f32[32,128,128]{2,1,0:T(8,128)} %x_hbm.1), custom_call_target="tpu_custom_call" | custom-call | flops 4 | bytes 4194304 | tf_op jit(solution)/shard_map/fetch/pallas_call | solution.py:423
  1.6 0.0 copy-done
  1.6 0.0 copy-start.1
  1.6 1.1 %moments.1.mine = f32[4,32,128]{2,1,0:T(8,128)S(1)} custom-call(f32[32]{0:T(128)S(1)} %copy-done, f32[32,128,128]{2,1,0:T(8,128)S(1)} %fetch.1.x.refs_2_.refs_0_), custom_call_target="tpu_custom_call" | custom-call | flops 2097152 | bytes 2097152 | tf_op jit(solution)/shard_map/moments/pallas_call | solution.py:433
  2.7 3.0 %collective-permute-start = (f32[4,32,128]{2,1,0:T(8,128)S(1)}, f32[4,32,128]{2,1,0:T(8,128)S(1)}, u32[]{:S(2)}, u32[]{:S(2)}) collective-permute-start(f32[4,32,128]{2,1,0:T(8,128)S(1)} %moments.1.mine), channel_id=1, source_target_pairs={{0,4},{4,0},{8,12},{12,8},{16,20},{20,16},{24,28},{28,24},{1,5},{5... | collective-permute-start | bytes 196616 | tf_op jit(solution)/shard_map/ppermute | solution.py:453
  5.7 0.0 copy-done.1
  5.7 2.4 %local.3 = (f32[10,128,128]{2,1,0:T(8,128)S(1)}, f32[10,8,128]{2,1,0:T(8,128)S(1)}, f32[5,32,128]{2,1,0:T(8,128)S(1)}, f32[7,32,128]{2,1,0:T(8,128)S(1)}, f32[7,...) custom-call(f32[32]{0:T(128)S(1)} %copy-done, f32[32]{0:T(128)S(1)} %copy-done.1, ...), custom_call_target="tpu_custom_call" | custom-call | flops 251658240 | bytes 1310720 | tf_op jit(solution)/shard_map/local/pallas_call | solution.py:471
  8.1 0.0 collective-permute-done.got
  8.2 2.0 %collective-permute-start.1 = (f32[3,32,128]{2,1,0:T(8,128)S(1)}, f32[3,32,128]{2,1,0:T(8,128)S(1)}, u32[]{:S(2)}, u32[]{:S(2)}) collective-permute-start(f32[3,32,128]{2,1,0:T(8,128)S(1)} %get-tuple-element.25.refs_4_.mine), channel_id=1, source_target_pairs={{0,8},{4,12},{8,0},{12,4},{16,24},{20,28},{24,16},{28,20},{1,9},{5... | collective-permute-start | bytes 147464 | tf_op jit(solution)/shard_map/ppermute | solution.py:453
  10.2 1.9 %local.4 = (f32[11,128,128]{2,1,0:T(8,128)S(1)}, f32[11,8,128]{2,1,0:T(8,128)S(1)}) custom-call(f32[32,128,128]{2,1,0:T(8,128)S(1)} %fetch.1.x.refs_2_.refs_0_, f32[7,32,128]{2,1,0:T(8,128)S(1)} %get-tuple-element.27.refs_1_, f32[8,32,128]{2,1,0:T(8,128)S(1)} %get-tuple-element.28.refs_2_, f32[32,8,128]{2,1,0:T(8,128)S(1)} %get-tuple-element.29.refs_3_, ...), custom_call_target="tpu_custom_call" | custom-call | flops 276824064 | bytes 1441792 | tf_op jit(solution)/shard_map/local/pallas_call | solution.py:471
  12.1 0.3 %collective-permute-done.1.got = f32[3,32,128]{2,1,0:T(8,128)S(1)} collective-permute-done((f32[3,32,128]{2,1,0:T(8,128)S(1)}, f32[3,32,128]{2,1,0:T(8,128)S(1)}, u32[]{:S(2)}, u32[]{:S(2)}) %collective-permute-start.1) | collective-permute-done | bytes 49184 | tf_op jit(solution)/shard_map/ppermute | solution.py:453
  12.4 3.0 %collective-permute-start.2 = (f32[2,32,128]{2,1,0:T(8,128)S(1)}, f32[2,32,128]{2,1,0:T(8,128)S(1)}, u32[]{:S(2)}, u32[]{:S(2)}) collective-permute-start(f32[2,32,128]{2,1,0:T(8,128)S(1)} %get-tuple-element.31.refs_4_), channel_id=1, source_target_pairs={{0,16},{4,20},{8,24},{12,28},{16,0},{20,4},{24,8},{28,12},{1,17},{... | collective-permute-start | bytes 98312 | tf_op jit(solution)/shard_map/ppermute | solution.py:453
  15.4 1.9 %local.5 = (f32[11,128,128]{2,1,0:T(8,128)S(1)}, f32[11,8,128]{2,1,0:T(8,128)S(1)}) custom-call(f32[32,128,128]{2,1,0:T(8,128)S(1)} %fetch.1.x.refs_2_.refs_0_, f32[7,32,128]{2,1,0:T(8,128)S(1)} %get-tuple-element.27.refs_1_, f32[8,32,128]{2,1,0:T(8,128)S(1)} %get-tuple-element.28.refs_2_, f32[32,8,128]{2,1,0:T(8,128)S(1)} %get-tuple-element.29.refs_3_, ...), custom_call_target="tpu_custom_call" | custom-call | flops 276824064 | bytes 1441792 | tf_op jit(solution)/shard_map/local/pallas_call | solution.py:471
  17.3 0.0 collective-permute-done.2.got
  17.3 0.2 middle.1
  17.5 0.1 collective-permute-start.3
  17.5 1.9 %collective-permute-start.4 = (f32[2,32,128]{2,1,0:T(8,128)S(1)}, f32[2,32,128]{2,1,0:T(8,128)S(1)}, u32[]{:S(2)}, u32[]{:S(2)}) collective-permute-start(f32[2,32,128]{2,1,0:T(8,128)S(1)} %get-tuple-element.36), channel_id=1, source_target_pairs={{0,2},{1,3},{2,0},{3,1},{4,6},{5,7},{6,4},{7,5},{8,10},{9,11},{10,... | collective-permute-start | bytes 98312 | tf_op jit(solution)/shard_map/ppermute | solution.py:507
  19.4 1.4 %collective-permute-start.5 = (f32[2,32,128]{2,1,0:T(8,128)S(1)}, f32[2,32,128]{2,1,0:T(8,128)S(1)}, u32[]{:S(2)}, u32[]{:S(2)}) collective-permute-start(f32[2,32,128]{2,1,0:T(8,128)S(1)} %get-tuple-element.37), channel_id=1, source_target_pairs={{0,3},{1,0},{2,1},{3,2},{4,7},{5,4},{6,5},{7,6},{8,11},{9,8},{10,9... | collective-permute-start | bytes 98312 | tf_op jit(solution)/shard_map/ppermute | solution.py:507
  20.8 1.2 %held.1.right = bf16[32,32,128]{2,1,0:T(8,128)(2,1)S(1)} custom-call(f32[32]{0:T(128)S(1)} %copy-done.1, f32[2,32,128]{2,1,0:T(8,128)S(1)} %collective-permute-done.2.got, f32[4,32,128]{2,1,0:T(8,128)S(1)} %get-tuple-element.32.held_in, f32[5,32,128]{2,1,0:T(8,128)S(1)} %get-tuple-element.23.refs_0_.refs_1_.ykeep, f32[7,32,128]{2,1,0:T(8,128)S(1)} %get-tuple-element.33.zkeep), custom_call_target="tpu_custom_call" | custom-call | flops 1638400 | bytes 409600 | tf_op jit(solution)/shard_map/held/pallas_call | solution.py:510
  22.0 0.0 collective-permute-done.3.rest_0_
  22.0 0.0 collective-permute-done.4.rest_1_
  22.0 0.3 %collective-permute-done.5.rest_2_ = f32[2,32,128]{2,1,0:T(8,128)S(1)} collective-permute-done((f32[2,32,128]{2,1,0:T(8,128)S(1)}, f32[2,32,128]{2,1,0:T(8,128)S(1)}, u32[]{:S(2)}, u32[]{:S(2)}) %collective-permute-start.5) | collective-permute-done | bytes 32800 | tf_op jit(solution)/shard_map/ppermute | solution.py:507
  22.4 1.6 %final.1 = f32[32,128,128]{2,1,0:T(8,128)} custom-call(bf16[32,32,128]{2,1,0:T(8,128)(2,1)S(1)} %held.1.right, f32[5,32,128]{2,1,0:T(8,128)S(1)} %get-tuple-element.23.refs_0_.refs_1_.ykeep, f32[7,32,128]{2,1,0:T(8,128)S(1)} %get-tuple-element.33.zkeep, f32[2,32,128]{2,1,0:T(8,128)S(1)} %collective-permute-done.3.rest_0_, ...), custom_call_target="tpu_custom_call" | custom-call | flops 33554432 | bytes 4194304 | tf_op jit(solution)/shard_map/final/pallas_call | solution.py:520
  (2 shorter events, 0.1 us)
Async XLA Ops:
  0.0 1.6 %copy-start = (f32[32]{0:T(128)S(1)}, f32[32]{0:T(128)}, u32[]{:S(2)}) copy-start(f32[32]{0:T(128)} %refs_0_.1) | copy-start | bytes 388
  1.6 4.1 %copy-start.1 = (f32[32]{0:T(128)S(1)}, f32[32]{0:T(128)}, u32[]{:S(2)}) copy-start(f32[32]{0:T(128)} %rates_z.1) | copy-start | bytes 388
  2.7 5.4 %collective-permute-start = (f32[4,32,128]{2,1,0:T(8,128)S(1)}, f32[4,32,128]{2,1,0:T(8,128)S(1)}, u32[]{:S(2)}, u32[]{:S(2)}) collective-permute-start(f32[4,32,128]{2,1,0:T(8,128)S(1)} %moments.1.mine), channel_id=1, source_target_pairs={{0,4},{4,0},{8,12},{12,8},{16,20},{20,16},{24,28},{28,24},{1,5},{5... | collective-permute-start | bytes 196616 | tf_op jit(solution)/shard_map/ppermute | solution.py:453
  8.2 4.2 %collective-permute-start.1 = (f32[3,32,128]{2,1,0:T(8,128)S(1)}, f32[3,32,128]{2,1,0:T(8,128)S(1)}, u32[]{:S(2)}, u32[]{:S(2)}) collective-permute-start(f32[3,32,128]{2,1,0:T(8,128)S(1)} %get-tuple-element.25.refs_4_.mine), channel_id=1, source_target_pairs={{0,8},{4,12},{8,0},{12,4},{16,24},{20,28},{24,16},{28,20},{1,9},{5... | collective-permute-start | bytes 147464 | tf_op jit(solution)/shard_map/ppermute | solution.py:453
  12.4 4.9 %collective-permute-start.2 = (f32[2,32,128]{2,1,0:T(8,128)S(1)}, f32[2,32,128]{2,1,0:T(8,128)S(1)}, u32[]{:S(2)}, u32[]{:S(2)}) collective-permute-start(f32[2,32,128]{2,1,0:T(8,128)S(1)} %get-tuple-element.31.refs_4_), channel_id=1, source_target_pairs={{0,16},{4,20},{8,24},{12,28},{16,0},{20,4},{24,8},{28,12},{1,17},{... | collective-permute-start | bytes 98312 | tf_op jit(solution)/shard_map/ppermute | solution.py:453
  17.5 4.6 %collective-permute-start.3 = (f32[2,32,128]{2,1,0:T(8,128)S(1)}, f32[2,32,128]{2,1,0:T(8,128)S(1)}, u32[]{:S(2)}, u32[]{:S(2)}) collective-permute-start(f32[2,32,128]{2,1,0:T(8,128)S(1)} %get-tuple-element.35), channel_id=1, source_target_pairs={{0,1},{1,2},{2,3},{3,0},{4,5},{5,6},{6,7},{7,4},{8,9},{9,10},{10,1... | collective-permute-start | bytes 98312 | tf_op jit(solution)/shard_map/ppermute | solution.py:507
  17.5 4.5 %collective-permute-start.4 = (f32[2,32,128]{2,1,0:T(8,128)S(1)}, f32[2,32,128]{2,1,0:T(8,128)S(1)}, u32[]{:S(2)}, u32[]{:S(2)}) collective-permute-start(f32[2,32,128]{2,1,0:T(8,128)S(1)} %get-tuple-element.36), channel_id=1, source_target_pairs={{0,2},{1,3},{2,0},{3,1},{4,6},{5,7},{6,4},{7,5},{8,10},{9,11},{10,... | collective-permute-start | bytes 98312 | tf_op jit(solution)/shard_map/ppermute | solution.py:507
  19.4 3.0 %collective-permute-start.5 = (f32[2,32,128]{2,1,0:T(8,128)S(1)}, f32[2,32,128]{2,1,0:T(8,128)S(1)}, u32[]{:S(2)}, u32[]{:S(2)}) collective-permute-start(f32[2,32,128]{2,1,0:T(8,128)S(1)} %get-tuple-element.37), channel_id=1, source_target_pairs={{0,3},{1,0},{2,1},{3,2},{4,7},{5,4},{6,5},{7,6},{8,11},{9,8},{10,9... | collective-permute-start | bytes 98312 | tf_op jit(solution)/shard_map/ppermute | solution.py:507

commit v4 on v3

--- a/solution.py
+++ b/solution.py
@@ -17,9 +17,14 @@
 CUTS = (0, 2, 5, 10, 16)
 
 
-def spread(rates, table):
-    for k in range(table.shape[0]):
-        table[pl.ds(k, 1), :] = jnp.full((1, table.shape[1]), rates[k], F32)
+def down_sublanes(rates, lanes):
+    planes = rates.shape[0]
+    row = jnp.broadcast_to(rates[...].reshape(1, planes), (planes, planes))
+    diagonal = lax.broadcasted_iota(jnp.int32, row.shape, 0) == lax.broadcasted_iota(
+        jnp.int32, row.shape, 1
+    )
+    column = jnp.sum(jnp.where(diagonal, row, 0.0), axis=1, keepdims=True)
+    return jnp.broadcast_to(column, (planes, lanes))
 
 
 class Line:
@@ -29,6 +34,7 @@
         sinh = jnp.sqrt(eps * (2.0 + eps))
         corner = rate * outer_weight
         self.m = m
+        self.growth = 1.0 + (eps + sinh)
         self.theta = jnp.log1p(eps + sinh)
         total = m * devices
         self.far = total + 1 - m * position
@@ -96,24 +102,24 @@
 def moments_kernel(devices, rates, x, out, table, up_rows, down_rows):
     planes, m, n = x.shape
     position = lax.axis_index("gy")
-    spread(rates, table)
-    line = Line(table[...], position, devices, m)
-    one = line.power(1)
-    eighth = line.power(8)
+    line = Line(down_sublanes(rates, n), position, devices, m)
+    one = 1.0 / line.growth
+    eighth = one * one
+    eighth = eighth * eighth
+    eighth = eighth * eighth
     across = line.power(m - 1)
     lower_scale, upper_scale = line.corner * line.is_first, line.corner * line.is_last
     turn_up, turn_down = line.power(2 * line.near + m + 1), line.power(2 * line.far - m - 1)
     table[...] = eighth
-    if True:
-        for k in range(planes):
-            ratio = jnp.broadcast_to(table[k : k + 1, :], (8, n))
-            up, down = x[k, 0:8, :], x[k, m - 8 : m, :]
-            for v in range(1, m // 8):
-                up = up * ratio + x[k, 8 * v : 8 * v + 8, :]
-                w = m - 8 - 8 * v
-                down = down * ratio + x[k, w : w + 8, :]
-            up_rows[k] = up
-            down_rows[k] = down
+    for k in range(planes):
+        ratio = jnp.broadcast_to(table[k : k + 1, :], (8, n))
+        rows = [x[k, v : v + 8, :] for v in range(0, m, 8)]
+        up, down = rows[0], rows[-1]
+        for ahead, behind in zip(rows[1:], rows[-2::-1]):
+            up = up * ratio + ahead
+            down = down * ratio + behind
+        up_rows[k] = up
+        down_rows[k] = down
     up, down = up_rows[:, 0, :], down_rows[:, 7, :]
     for s in range(1, 8):
         up = up * one + up_rows[:, s, :]
@@ -143,10 +149,9 @@
     return phi, chi
 
 
-def make_tables(dev_y, dev_z, rates_y, rates_z, m, n, ykeep, zkeep, ytab, ztab, nz, table):
+def make_tables(dev_y, dev_z, rates_y, rates_z, m, n, ykeep, zkeep, ytab, ztab, nz):
     pos_y, pos_z = lax.axis_index("gy"), lax.axis_index("gz")
-    spread(rates_y, table)
-    y = Line(table[...], pos_y, dev_y, m)
+    y = Line(down_sublanes(rates_y, m), pos_y, dev_y, m)
     y.vectors()
     for i, row in enumerate((y.get_up, y.get_down, y.side * y.head, y.side * y.tail, y.theta)):
         ykeep[i] = row
@@ -154,8 +159,7 @@
         (y.theta, y.cut_far, y.cut_near, y.phi * y.weight, y.chi * y.weight, y.mid, y.side)
     ):
         ytab[i] = row
-    spread(rates_z, table)
-    z = Line(table[...], pos_z, dev_z, n)
+    z = Line(down_sublanes(rates_z, n), pos_z, dev_z, n)
     z.vectors()
     for i, row in enumerate(
         (z.get_up, z.get_down, z.side * z.head, z.side * z.tail, z.power(n), z.send_up, z.send_down)
@@ -173,9 +177,9 @@
 
 def local_kernel(dev_y, dev_z, lo, hi, *refs):
     if lo == 0:
-        rates_y, rates_z, x, out, sums, ykeep, zkeep, ytab, ztab, nz, table = refs[:11]
+        rates_y, rates_z, x, out, sums, ykeep, zkeep, ytab, ztab, nz = refs[:10]
         make_tables(
-            dev_y, dev_z, rates_y, rates_z, x.shape[1], x.shape[2], ykeep, zkeep, ytab, ztab, nz, table
+            dev_y, dev_z, rates_y, rates_z, x.shape[1], x.shape[2], ykeep, zkeep, ytab, ztab, nz
         )
     else:
         x, ytab, ztab, nz, _, out, sums = refs[:7]
@@ -352,9 +356,8 @@
         send[1] = jnp.where(ahead, tail, head)
 
 
-def held_kernel(stage, dev_z, rates_z, got, held_in, ykeep, zkeep, right_split, table, right):
-    spread(rates_z, table)
-    z = Line(table[...], lax.axis_index("gz"), dev_z, table.shape[1])
+def held_kernel(stage, dev_z, rates_z, got, held_in, ykeep, zkeep, right_split, right):
+    z = Line(down_sublanes(rates_z, right.shape[2]), lax.axis_index("gz"), dev_z, right.shape[2])
     z.vectors()
     for i, row in enumerate(along_lanes(z, arrivals(stage, ykeep.shape[2], ykeep, got, held_in))):
         right[:, i, :] = row
@@ -405,7 +408,6 @@
 def per_device(x, rates_y, rates_z):
     planes, m, n = x.shape
     dev_y, dev_z = lax.axis_size("gy"), lax.axis_size("gz")
-    smem = pl.BlockSpec(memory_space=pltpu.SMEM)
     whole = pl.BlockSpec(memory_space=pltpu.VMEM)
 
     def params():
@@ -432,7 +434,7 @@
     )(x)
     send = pl.pallas_call(
         functools.partial(moments_kernel, dev_y),
-        in_specs=[smem, whole],
+        in_specs=[whole, whole],
         out_specs=whole,
         out_shape=shape(4, planes, n),
         scratch_shapes=[
@@ -455,7 +457,7 @@
         outs = [shape(hi - lo, m, n), shape(hi - lo, 8, m)]
         if first:
             given = (rates_y, rates_z, x)
-            in_specs = [smem, smem, whole]
+            in_specs = [whole] * 3
             outs += [
                 shape(5, planes, m),
                 shape(7, planes, n),
@@ -463,18 +465,15 @@
                 shape(8, planes, n),
                 shape(planes, 8, n),
             ]
-            scratch = [pltpu.VMEM((planes, n), F32)]
         else:
             given = (x, *tables, send)
             in_specs = [whole] * 5
-            scratch = []
         part, piece, *rest = pl.pallas_call(
             functools.partial(local_kernel, dev_y, dev_z, lo, hi),
             in_specs=in_specs,
             out_specs=[whole] * len(outs),
             out_shape=outs,
-            scratch_shapes=scratch
-            + [pltpu.VMEM((2, m, n), F32)],
+            scratch_shapes=[pltpu.VMEM((2, m, n), F32)],
             compiler_params=params(),
             cost_estimate=cost(12 * (hi - lo) * m * m * n, 8 * (hi - lo) * m * n),
             name="local",
@@ -509,10 +508,10 @@
     ]
     held = pl.pallas_call(
         functools.partial(held_kernel, stages - 1, dev_z),
-        in_specs=[smem, whole, whole, whole, whole],
+        in_specs=[whole] * 5,
         out_specs=whole,
         out_shape=jax.ShapeDtypeStruct((planes, 32, n), BF16),
-        scratch_shapes=[pltpu.VMEM((planes, n), F32), pltpu.VMEM((planes, 8, n), F32)],
+        scratch_shapes=[pltpu.VMEM((planes, 8, n), F32)],
         compiler_params=params(),
         cost_estimate=cost(planes * n * 400, planes * n * 100),
         name="held",

time: 24.1 us -> 23.7 us (0.983)
  Pallas kernels: 11.9 us -> 10.4 us
  waiting for transfers between devices: 0.63 us -> 1.37 us
  starting transfers between devices: 11.3 us -> 11.6 us
    pallas_call x3, Pallas kernels: 6.18 us -> 5.65 us  [per_device(): pl.pallas_call(functools.partial(local_kernel, dev_y, dev_z, lo, hi), in_...]
    pallas_call x1, Pallas kernels: 1.24 us -> 0.74 us  [per_device(): pl.pallas_call(functools.partial(held_kernel, stages - 1, dev_z), in_spec...]
    ppermute x3, waiting for transfers between devices: 0.33 us -> 0.83 us  [per_device(): lax.ppermute(send, 'gz', [(i, (i + by + 1) % dev_z) for i in range(dev_z)])]
    pallas_call x1, Pallas kernels: 1.08 us -> 0.61 us  [per_device(): pl.pallas_call(functools.partial(moments_kernel, dev_y), in_specs=[whole,...]
    ppermute x3, starting transfers between devices: 7.98 us -> 8.27 us  [per_device(): got = lax.ppermute(send, 'gy', [(i, i ^ 1 << stage) for i in range(dev_y)])]
    ppermute x3, waiting for transfers between devices: 0.29 us -> 0.54 us  [per_device(): got = lax.ppermute(send, 'gy', [(i, i ^ 1 << stage) for i in range(dev_y)])]
  transfers between devices with their start and end apart: 6 -> 6, of which waited for: 2 -> 3; matrix products, arithmetic and copies ran while one was open for 0% -> 0% of each run, Pallas kernels for 31% -> 27%
where the time goes in v4:
time: 23.7 us; the launch traced here: 23.5 us
  starting transfers between devices  11.6 us (49%)
  Pallas kernels  10.4 us (44%)
  waiting for transfers between devices  1.37 us (6%)
    ppermute x3, starting transfers between devices, per_device(): got = lax.ppermute(send, 'gy', [(i, i ^ 1 << stage) for i in range(dev_y)])  8.27 us
    pallas_call x3, Pallas kernels, per_device(): pl.pallas_call(functools.partial(local_kernel, dev_y, dev_z, lo, hi), in_...  5.65 us
    ppermute x3, starting transfers between devices, per_device(): lax.ppermute(send, 'gz', [(i, (i + by + 1) % dev_z) for i in range(dev_z)])  3.31 us
    pallas_call x1, Pallas kernels, per_device(): pl.pallas_call(functools.partial(final_kernel, dev_z, bounds), in_specs=[...  1.61 us
    pallas_call x1, Pallas kernels, per_device(): pl.pallas_call(fetch_kernel, in_specs=[hbm], out_specs=whole, out_shape=s...  1.58 us
    ppermute x3, waiting for transfers between devices, per_device(): lax.ppermute(send, 'gz', [(i, (i + by + 1) % dev_z) for i in range(dev_z)])  0.83 us
    pallas_call x1, Pallas kernels, per_device(): pl.pallas_call(functools.partial(held_kernel, stages - 1, dev_z), in_spec...  0.74 us
    pallas_call x1, Pallas kernels, per_device(): pl.pallas_call(functools.partial(moments_kernel, dev_y), in_specs=[whole,...  0.61 us
  transfers between devices with their start and end apart: 6, of which 3 were waited for; matrix products, arithmetic and copies ran while one was open for 0% of the time, Pallas kernels for 27%

profile of v4, /device:TPU:0, one launch (start us, length us, event | category | flops | bytes accessed | tf_op | source)
XLA Modules:
  0.0 23.5 jit_solution(8628419571602507580)
XLA Ops:
  0.0 0.0 copy-start
  0.0 1.6 %fetch.1.x.refs_2_.refs_0_ = f32[32,128,128]{2,1,0:T(8,128)S(1)} custom-call(f32[32,128,128]{2,1,0:T(8,128)} %x_hbm.1), custom_call_target="tpu_custom_call" | custom-call | flops 4 | bytes 4194304 | tf_op jit(solution)/shard_map/fetch/pallas_call | solution.py:425
  1.6 0.0 copy-done
  1.6 0.0 copy-start.1
  1.6 0.6 %moments.1.mine = f32[4,32,128]{2,1,0:T(8,128)S(1)} custom-call(f32[32]{0:T(128)S(1)} %copy-done, f32[32,128,128]{2,1,0:T(8,128)S(1)} %fetch.1.x.refs_2_.refs_0_), custom_call_target="tpu_custom_call" | custom-call | flops 2097152 | bytes 2097152 | tf_op jit(solution)/shard_map/moments/pallas_call | solution.py:435
  2.2 3.0 %collective-permute-start = (f32[4,32,128]{2,1,0:T(8,128)S(1)}, f32[4,32,128]{2,1,0:T(8,128)S(1)}, u32[]{:S(2)}, u32[]{:S(2)}) collective-permute-start(f32[4,32,128]{2,1,0:T(8,128)S(1)} %moments.1.mine), channel_id=1, source_target_pairs={{0,4},{4,0},{8,12},{12,8},{16,20},{20,16},{24,28},{28,24},{1,5},{5... | collective-permute-start | bytes 196616 | tf_op jit(solution)/shard_map/ppermute | solution.py:455
  5.3 0.0 copy-done.1
  5.3 1.9 %local.3 = (f32[10,128,128]{2,1,0:T(8,128)S(1)}, f32[10,8,128]{2,1,0:T(8,128)S(1)}, f32[5,32,128]{2,1,0:T(8,128)S(1)}, f32[7,32,128]{2,1,0:T(8,128)S(1)}, f32[7,...) custom-call(f32[32]{0:T(128)S(1)} %copy-done, f32[32]{0:T(128)S(1)} %copy-done.1, ...), custom_call_target="tpu_custom_call" | custom-call | flops 251658240 | bytes 1310720 | tf_op jit(solution)/shard_map/local/pallas_call | solution.py:471
  7.1 0.4 %collective-permute-done.got = f32[4,32,128]{2,1,0:T(8,128)S(1)} collective-permute-done((f32[4,32,128]{2,1,0:T(8,128)S(1)}, f32[4,32,128]{2,1,0:T(8,128)S(1)}, u32[]{:S(2)}, u32[]{:S(2)}) %collective-permute-start) | collective-permute-done | bytes 65568 | tf_op jit(solution)/shard_map/ppermute | solution.py:455
  7.5 2.1 %collective-permute-start.1 = (f32[3,32,128]{2,1,0:T(8,128)S(1)}, f32[3,32,128]{2,1,0:T(8,128)S(1)}, u32[]{:S(2)}, u32[]{:S(2)}) collective-permute-start(f32[3,32,128]{2,1,0:T(8,128)S(1)} %get-tuple-element.25.refs_4_.mine), channel_id=1, source_target_pairs={{0,8},{4,12},{8,0},{12,4},{16,24},{20,28},{24,16},{28,20},{1,9},{5... | collective-permute-start | bytes 147464 | tf_op jit(solution)/shard_map/ppermute | solution.py:455
  9.7 1.9 %local.4 = (f32[11,128,128]{2,1,0:T(8,128)S(1)}, f32[11,8,128]{2,1,0:T(8,128)S(1)}) custom-call(f32[32,128,128]{2,1,0:T(8,128)S(1)} %fetch.1.x.refs_2_.refs_0_, f32[7,32,128]{2,1,0:T(8,128)S(1)} %get-tuple-element.27.refs_1_, f32[8,32,128]{2,1,0:T(8,128)S(1)} %get-tuple-element.28.refs_2_, f32[32,8,128]{2,1,0:T(8,128)S(1)} %get-tuple-element.29.refs_3_, ...), custom_call_target="tpu_custom_call" | custom-call | flops 276824064 | bytes 1441792 | tf_op jit(solution)/shard_map/local/pallas_call | solution.py:471
  11.6 0.2 collective-permute-done.1.got
  11.8 3.1 %collective-permute-start.2 = (f32[2,32,128]{2,1,0:T(8,128)S(1)}, f32[2,32,128]{2,1,0:T(8,128)S(1)}, u32[]{:S(2)}, u32[]{:S(2)}) collective-permute-start(f32[2,32,128]{2,1,0:T(8,128)S(1)} %get-tuple-element.31.refs_4_), channel_id=1, source_target_pairs={{0,16},{4,20},{8,24},{12,28},{16,0},{20,4},{24,8},{28,12},{1,17},{... | collective-permute-start | bytes 98312 | tf_op jit(solution)/shard_map/ppermute | solution.py:455
  14.9 1.9 %local.5 = (f32[11,128,128]{2,1,0:T(8,128)S(1)}, f32[11,8,128]{2,1,0:T(8,128)S(1)}) custom-call(f32[32,128,128]{2,1,0:T(8,128)S(1)} %fetch.1.x.refs_2_.refs_0_, f32[7,32,128]{2,1,0:T(8,128)S(1)} %get-tuple-element.27.refs_1_, f32[8,32,128]{2,1,0:T(8,128)S(1)} %get-tuple-element.28.refs_2_, f32[32,8,128]{2,1,0:T(8,128)S(1)} %get-tuple-element.29.refs_3_, ...), custom_call_target="tpu_custom_call" | custom-call | flops 276824064 | bytes 1441792 | tf_op jit(solution)/shard_map/local/pallas_call | solution.py:471
  16.8 0.0 collective-permute-done.2.got
  16.8 0.2 middle.1
  17.0 0.1 collective-permute-start.3
  17.1 1.9 %collective-permute-start.4 = (f32[2,32,128]{2,1,0:T(8,128)S(1)}, f32[2,32,128]{2,1,0:T(8,128)S(1)}, u32[]{:S(2)}, u32[]{:S(2)}) collective-permute-start(f32[2,32,128]{2,1,0:T(8,128)S(1)} %get-tuple-element.36), channel_id=1, source_target_pairs={{0,2},{1,3},{2,0},{3,1},{4,6},{5,7},{6,4},{7,5},{8,10},{9,11},{10,... | collective-permute-start | bytes 98312 | tf_op jit(solution)/shard_map/ppermute | solution.py:506
  18.9 1.4 %collective-permute-start.5 = (f32[2,32,128]{2,1,0:T(8,128)S(1)}, f32[2,32,128]{2,1,0:T(8,128)S(1)}, u32[]{:S(2)}, u32[]{:S(2)}) collective-permute-start(f32[2,32,128]{2,1,0:T(8,128)S(1)} %get-tuple-element.37), channel_id=1, source_target_pairs={{0,3},{1,0},{2,1},{3,2},{4,7},{5,4},{6,5},{7,6},{8,11},{9,8},{10,9... | collective-permute-start | bytes 98312 | tf_op jit(solution)/shard_map/ppermute | solution.py:506
  20.3 0.7 %held.1.right = bf16[32,32,128]{2,1,0:T(8,128)(2,1)S(1)} custom-call(f32[32]{0:T(128)S(1)} %copy-done.1, f32[2,32,128]{2,1,0:T(8,128)S(1)} %collective-permute-done.2.got, f32[4,32,128]{2,1,0:T(8,128)S(1)} %get-tuple-element.32.held_in, f32[5,32,128]{2,1,0:T(8,128)S(1)} %get-tuple-element.23.refs_0_.refs_1_.ykeep, f32[7,32,128]{2,1,0:T(8,128)S(1)} %get-tuple-element.33.zkeep), custom_call_target="tpu_custom_call" | custom-call | flops 1638400 | bytes 409600 | tf_op jit(solution)/shard_map/held/pallas_call | solution.py:509
  21.1 0.0 collective-permute-done.3.rest_0_
  21.1 0.0 collective-permute-done.4.rest_1_
  21.1 0.8 %collective-permute-done.5.rest_2_ = f32[2,32,128]{2,1,0:T(8,128)S(1)} collective-permute-done((f32[2,32,128]{2,1,0:T(8,128)S(1)}, f32[2,32,128]{2,1,0:T(8,128)S(1)}, u32[]{:S(2)}, u32[]{:S(2)}) %collective-permute-start.5) | collective-permute-done | bytes 32800 | tf_op jit(solution)/shard_map/ppermute | solution.py:506
  21.9 1.6 %final.1 = f32[32,128,128]{2,1,0:T(8,128)} custom-call(bf16[32,32,128]{2,1,0:T(8,128)(2,1)S(1)} %held.1.right, f32[5,32,128]{2,1,0:T(8,128)S(1)} %get-tuple-element.23.refs_0_.refs_1_.ykeep, f32[7,32,128]{2,1,0:T(8,128)S(1)} %get-tuple-element.33.zkeep, f32[2,32,128]{2,1,0:T(8,128)S(1)} %collective-permute-done.3.rest_0_, ...), custom_call_target="tpu_custom_call" | custom-call | flops 33554432 | bytes 4194304 | tf_op jit(solution)/shard_map/final/pallas_call | solution.py:519
  (2 shorter events, 0.1 us)
Async XLA Ops:
  0.0 1.6 %copy-start = (f32[32]{0:T(128)S(1)}, f32[32]{0:T(128)}, u32[]{:S(2)}) copy-start(f32[32]{0:T(128)} %refs_0_.1) | copy-start | bytes 388
  1.6 3.7 %copy-start.1 = (f32[32]{0:T(128)S(1)}, f32[32]{0:T(128)}, u32[]{:S(2)}) copy-start(f32[32]{0:T(128)} %rates_z.1) | copy-start | bytes 388
  2.2 5.3 %collective-permute-start = (f32[4,32,128]{2,1,0:T(8,128)S(1)}, f32[4,32,128]{2,1,0:T(8,128)S(1)}, u32[]{:S(2)}, u32[]{:S(2)}) collective-permute-start(f32[4,32,128]{2,1,0:T(8,128)S(1)} %moments.1.mine), channel_id=1, source_target_pairs={{0,4},{4,0},{8,12},{12,8},{16,20},{20,16},{24,28},{28,24},{1,5},{5... | collective-permute-start | bytes 196616 | tf_op jit(solution)/shard_map/ppermute | solution.py:455
  7.5 4.2 %collective-permute-start.1 = (f32[3,32,128]{2,1,0:T(8,128)S(1)}, f32[3,32,128]{2,1,0:T(8,128)S(1)}, u32[]{:S(2)}, u32[]{:S(2)}) collective-permute-start(f32[3,32,128]{2,1,0:T(8,128)S(1)} %get-tuple-element.25.refs_4_.mine), channel_id=1, source_target_pairs={{0,8},{4,12},{8,0},{12,4},{16,24},{20,28},{24,16},{28,20},{1,9},{5... | collective-permute-start | bytes 147464 | tf_op jit(solution)/shard_map/ppermute | solution.py:455
  11.8 5.0 %collective-permute-start.2 = (f32[2,32,128]{2,1,0:T(8,128)S(1)}, f32[2,32,128]{2,1,0:T(8,128)S(1)}, u32[]{:S(2)}, u32[]{:S(2)}) collective-permute-start(f32[2,32,128]{2,1,0:T(8,128)S(1)} %get-tuple-element.31.refs_4_), channel_id=1, source_target_pairs={{0,16},{4,20},{8,24},{12,28},{16,0},{20,4},{24,8},{28,12},{1,17},{... | collective-permute-start | bytes 98312 | tf_op jit(solution)/shard_map/ppermute | solution.py:455
  17.0 4.1 %collective-permute-start.3 = (f32[2,32,128]{2,1,0:T(8,128)S(1)}, f32[2,32,128]{2,1,0:T(8,128)S(1)}, u32[]{:S(2)}, u32[]{:S(2)}) collective-permute-start(f32[2,32,128]{2,1,0:T(8,128)S(1)} %get-tuple-element.35), channel_id=1, source_target_pairs={{0,1},{1,2},{2,3},{3,0},{4,5},{5,6},{6,7},{7,4},{8,9},{9,10},{10,1... | collective-permute-start | bytes 98312 | tf_op jit(solution)/shard_map/ppermute | solution.py:506
  17.1 4.0 %collective-permute-start.4 = (f32[2,32,128]{2,1,0:T(8,128)S(1)}, f32[2,32,128]{2,1,0:T(8,128)S(1)}, u32[]{:S(2)}, u32[]{:S(2)}) collective-permute-start(f32[2,32,128]{2,1,0:T(8,128)S(1)} %get-tuple-element.36), channel_id=1, source_target_pairs={{0,2},{1,3},{2,0},{3,1},{4,6},{5,7},{6,4},{7,5},{8,10},{9,11},{10,... | collective-permute-start | bytes 98312 | tf_op jit(solution)/shard_map/ppermute | solution.py:506
  18.9 3.0 %collective-permute-start.5 = (f32[2,32,128]{2,1,0:T(8,128)S(1)}, f32[2,32,128]{2,1,0:T(8,128)S(1)}, u32[]{:S(2)}, u32[]{:S(2)}) collective-permute-start(f32[2,32,128]{2,1,0:T(8,128)S(1)} %get-tuple-element.37), channel_id=1, source_target_pairs={{0,3},{1,0},{2,1},{3,2},{4,7},{5,4},{6,5},{7,6},{8,11},{9,8},{10,9... | collective-permute-start | bytes 98312 | tf_op jit(solution)/shard_map/ppermute | solution.py:506

commit v5 on v4

--- a/solution.py
+++ b/solution.py
@@ -427,7 +427,7 @@
         in_specs=[hbm],
         out_specs=whole,
         out_shape=shape(planes, m, n),
-        scratch_shapes=[pltpu.SemaphoreType.DMA((8,))],
+        scratch_shapes=[pltpu.SemaphoreType.DMA((2,))],
         compiler_params=pltpu.CompilerParams(vmem_limit_bytes=FETCH_VMEM),
         cost_estimate=cost(4, 8 * cells),
         name="fetch",

time: 23.7 us -> 23.6 us (level)
  no operation moved by 1% of the time
where the time goes in v5:
time: 23.6 us; the launch traced here: 23.5 us
  starting transfers between devices  11.6 us (49%)
  Pallas kernels  10.4 us (44%)
  waiting for transfers between devices  1.37 us (6%)
    ppermute x3, starting transfers between devices, per_device(): got = lax.ppermute(send, 'gy', [(i, i ^ 1 << stage) for i in range(dev_y)])  8.27 us
    pallas_call x3, Pallas kernels, per_device(): pl.pallas_call(functools.partial(local_kernel, dev_y, dev_z, lo, hi), in_...  5.65 us
    ppermute x3, starting transfers between devices, per_device(): lax.ppermute(send, 'gz', [(i, (i + by + 1) % dev_z) for i in range(dev_z)])  3.31 us
    pallas_call x1, Pallas kernels, per_device(): pl.pallas_call(functools.partial(final_kernel, dev_z, bounds), in_specs=[...  1.61 us
    pallas_call x1, Pallas kernels, per_device(): pl.pallas_call(fetch_kernel, in_specs=[hbm], out_specs=whole, out_shape=s...  1.57 us
    ppermute x3, waiting for transfers between devices, per_device(): lax.ppermute(send, 'gz', [(i, (i + by + 1) % dev_z) for i in range(dev_z)])  0.83 us
    pallas_call x1, Pallas kernels, per_device(): pl.pallas_call(functools.partial(held_kernel, stages - 1, dev_z), in_spec...  0.74 us
    pallas_call x1, Pallas kernels, per_device(): pl.pallas_call(functools.partial(moments_kernel, dev_y), in_specs=[whole,...  0.61 us
  transfers between devices with their start and end apart: 6, of which 3 were waited for; matrix products, arithmetic and copies ran while one was open for 0% of the time, Pallas kernels for 27%

profile of v5, /device:TPU:0, one launch (start us, length us, event | category | flops | bytes accessed | tf_op | source)
XLA Modules:
  0.0 23.5 jit_solution(2873150610767508672)
XLA Ops:
  0.0 0.0 copy-start
  0.0 1.6 %fetch.1.x.refs_2_.refs_0_ = f32[32,128,128]{2,1,0:T(8,128)S(1)} custom-call(f32[32,128,128]{2,1,0:T(8,128)} %x_hbm.1), custom_call_target="tpu_custom_call" | custom-call | flops 4 | bytes 4194304 | tf_op jit(solution)/shard_map/fetch/pallas_call | solution.py:425
  1.6 0.0 copy-done
  1.6 0.0 copy-start.1
  1.6 0.6 %moments.1.mine = f32[4,32,128]{2,1,0:T(8,128)S(1)} custom-call(f32[32]{0:T(128)S(1)} %copy-done, f32[32,128,128]{2,1,0:T(8,128)S(1)} %fetch.1.x.refs_2_.refs_0_), custom_call_target="tpu_custom_call" | custom-call | flops 2097152 | bytes 2097152 | tf_op jit(solution)/shard_map/moments/pallas_call | solution.py:435
  2.2 3.0 %collective-permute-start = (f32[4,32,128]{2,1,0:T(8,128)S(1)}, f32[4,32,128]{2,1,0:T(8,128)S(1)}, u32[]{:S(2)}, u32[]{:S(2)}) collective-permute-start(f32[4,32,128]{2,1,0:T(8,128)S(1)} %moments.1.mine), channel_id=1, source_target_pairs={{0,4},{4,0},{8,12},{12,8},{16,20},{20,16},{24,28},{28,24},{1,5},{5... | collective-permute-start | bytes 196616 | tf_op jit(solution)/shard_map/ppermute | solution.py:455
  5.3 0.0 copy-done.1
  5.3 1.9 %local.3 = (f32[10,128,128]{2,1,0:T(8,128)S(1)}, f32[10,8,128]{2,1,0:T(8,128)S(1)}, f32[5,32,128]{2,1,0:T(8,128)S(1)}, f32[7,32,128]{2,1,0:T(8,128)S(1)}, f32[7,...) custom-call(f32[32]{0:T(128)S(1)} %copy-done, f32[32]{0:T(128)S(1)} %copy-done.1, ...), custom_call_target="tpu_custom_call" | custom-call | flops 251658240 | bytes 1310720 | tf_op jit(solution)/shard_map/local/pallas_call | solution.py:471
  7.1 0.4 %collective-permute-done.got = f32[4,32,128]{2,1,0:T(8,128)S(1)} collective-permute-done((f32[4,32,128]{2,1,0:T(8,128)S(1)}, f32[4,32,128]{2,1,0:T(8,128)S(1)}, u32[]{:S(2)}, u32[]{:S(2)}) %collective-permute-start) | collective-permute-done | bytes 65568 | tf_op jit(solution)/shard_map/ppermute | solution.py:455
  7.5 2.1 %collective-permute-start.1 = (f32[3,32,128]{2,1,0:T(8,128)S(1)}, f32[3,32,128]{2,1,0:T(8,128)S(1)}, u32[]{:S(2)}, u32[]{:S(2)}) collective-permute-start(f32[3,32,128]{2,1,0:T(8,128)S(1)} %get-tuple-element.25.refs_4_.mine), channel_id=1, source_target_pairs={{0,8},{4,12},{8,0},{12,4},{16,24},{20,28},{24,16},{28,20},{1,9},{5... | collective-permute-start | bytes 147464 | tf_op jit(solution)/shard_map/ppermute | solution.py:455
  9.7 1.9 %local.4 = (f32[11,128,128]{2,1,0:T(8,128)S(1)}, f32[11,8,128]{2,1,0:T(8,128)S(1)}) custom-call(f32[32,128,128]{2,1,0:T(8,128)S(1)} %fetch.1.x.refs_2_.refs_0_, f32[7,32,128]{2,1,0:T(8,128)S(1)} %get-tuple-element.27.refs_1_, f32[8,32,128]{2,1,0:T(8,128)S(1)} %get-tuple-element.28.refs_2_, f32[32,8,128]{2,1,0:T(8,128)S(1)} %get-tuple-element.29.refs_3_, ...), custom_call_target="tpu_custom_call" | custom-call | flops 276824064 | bytes 1441792 | tf_op jit(solution)/shard_map/local/pallas_call | solution.py:471
  11.6 0.2 collective-permute-done.1.got
  11.8 3.1 %collective-permute-start.2 = (f32[2,32,128]{2,1,0:T(8,128)S(1)}, f32[2,32,128]{2,1,0:T(8,128)S(1)}, u32[]{:S(2)}, u32[]{:S(2)}) collective-permute-start(f32[2,32,128]{2,1,0:T(8,128)S(1)} %get-tuple-element.31.refs_4_), channel_id=1, source_target_pairs={{0,16},{4,20},{8,24},{12,28},{16,0},{20,4},{24,8},{28,12},{1,17},{... | collective-permute-start | bytes 98312 | tf_op jit(solution)/shard_map/ppermute | solution.py:455
  14.9 1.9 %local.5 = (f32[11,128,128]{2,1,0:T(8,128)S(1)}, f32[11,8,128]{2,1,0:T(8,128)S(1)}) custom-call(f32[32,128,128]{2,1,0:T(8,128)S(1)} %fetch.1.x.refs_2_.refs_0_, f32[7,32,128]{2,1,0:T(8,128)S(1)} %get-tuple-element.27.refs_1_, f32[8,32,128]{2,1,0:T(8,128)S(1)} %get-tuple-element.28.refs_2_, f32[32,8,128]{2,1,0:T(8,128)S(1)} %get-tuple-element.29.refs_3_, ...), custom_call_target="tpu_custom_call" | custom-call | flops 276824064 | bytes 1441792 | tf_op jit(solution)/shard_map/local/pallas_call | solution.py:471
  16.8 0.0 collective-permute-done.2.got
  16.8 0.2 middle.1
  17.0 0.1 collective-permute-start.3
  17.0 1.9 %collective-permute-start.4 = (f32[2,32,128]{2,1,0:T(8,128)S(1)}, f32[2,32,128]{2,1,0:T(8,128)S(1)}, u32[]{:S(2)}, u32[]{:S(2)}) collective-permute-start(f32[2,32,128]{2,1,0:T(8,128)S(1)} %get-tuple-element.36), channel_id=1, source_target_pairs={{0,2},{1,3},{2,0},{3,1},{4,6},{5,7},{6,4},{7,5},{8,10},{9,11},{10,... | collective-permute-start | bytes 98312 | tf_op jit(solution)/shard_map/ppermute | solution.py:506
  18.9 1.4 %collective-permute-start.5 = (f32[2,32,128]{2,1,0:T(8,128)S(1)}, f32[2,32,128]{2,1,0:T(8,128)S(1)}, u32[]{:S(2)}, u32[]{:S(2)}) collective-permute-start(f32[2,32,128]{2,1,0:T(8,128)S(1)} %get-tuple-element.37), channel_id=1, source_target_pairs={{0,3},{1,0},{2,1},{3,2},{4,7},{5,4},{6,5},{7,6},{8,11},{9,8},{10,9... | collective-permute-start | bytes 98312 | tf_op jit(solution)/shard_map/ppermute | solution.py:506
  20.3 0.7 %held.1.right = bf16[32,32,128]{2,1,0:T(8,128)(2,1)S(1)} custom-call(f32[32]{0:T(128)S(1)} %copy-done.1, f32[2,32,128]{2,1,0:T(8,128)S(1)} %collective-permute-done.2.got, f32[4,32,128]{2,1,0:T(8,128)S(1)} %get-tuple-element.32.held_in, f32[5,32,128]{2,1,0:T(8,128)S(1)} %get-tuple-element.23.refs_0_.refs_1_.ykeep, f32[7,32,128]{2,1,0:T(8,128)S(1)} %get-tuple-element.33.zkeep), custom_call_target="tpu_custom_call" | custom-call | flops 1638400 | bytes 409600 | tf_op jit(solution)/shard_map/held/pallas_call | solution.py:509
  21.0 0.0 collective-permute-done.3.rest_0_
  21.1 0.0 collective-permute-done.4.rest_1_
  21.1 0.8 %collective-permute-done.5.rest_2_ = f32[2,32,128]{2,1,0:T(8,128)S(1)} collective-permute-done((f32[2,32,128]{2,1,0:T(8,128)S(1)}, f32[2,32,128]{2,1,0:T(8,128)S(1)}, u32[]{:S(2)}, u32[]{:S(2)}) %collective-permute-start.5) | collective-permute-done | bytes 32800 | tf_op jit(solution)/shard_map/ppermute | solution.py:506
  21.9 1.6 %final.1 = f32[32,128,128]{2,1,0:T(8,128)} custom-call(bf16[32,32,128]{2,1,0:T(8,128)(2,1)S(1)} %held.1.right, f32[5,32,128]{2,1,0:T(8,128)S(1)} %get-tuple-element.23.refs_0_.refs_1_.ykeep, f32[7,32,128]{2,1,0:T(8,128)S(1)} %get-tuple-element.33.zkeep, f32[2,32,128]{2,1,0:T(8,128)S(1)} %collective-permute-done.3.rest_0_, ...), custom_call_target="tpu_custom_call" | custom-call | flops 33554432 | bytes 4194304 | tf_op jit(solution)/shard_map/final/pallas_call | solution.py:519
  (2 shorter events, 0.1 us)
Async XLA Ops:
  0.0 1.6 %copy-start = (f32[32]{0:T(128)S(1)}, f32[32]{0:T(128)}, u32[]{:S(2)}) copy-start(f32[32]{0:T(128)} %refs_0_.1) | copy-start | bytes 388
  1.6 3.7 %copy-start.1 = (f32[32]{0:T(128)S(1)}, f32[32]{0:T(128)}, u32[]{:S(2)}) copy-start(f32[32]{0:T(128)} %rates_z.1) | copy-start | bytes 388
  2.2 5.3 %collective-permute-start = (f32[4,32,128]{2,1,0:T(8,128)S(1)}, f32[4,32,128]{2,1,0:T(8,128)S(1)}, u32[]{:S(2)}, u32[]{:S(2)}) collective-permute-start(f32[4,32,128]{2,1,0:T(8,128)S(1)} %moments.1.mine), channel_id=1, source_target_pairs={{0,4},{4,0},{8,12},{12,8},{16,20},{20,16},{24,28},{28,24},{1,5},{5... | collective-permute-start | bytes 196616 | tf_op jit(solution)/shard_map/ppermute | solution.py:455
  7.5 4.2 %collective-permute-start.1 = (f32[3,32,128]{2,1,0:T(8,128)S(1)}, f32[3,32,128]{2,1,0:T(8,128)S(1)}, u32[]{:S(2)}, u32[]{:S(2)}) collective-permute-start(f32[3,32,128]{2,1,0:T(8,128)S(1)} %get-tuple-element.25.refs_4_.mine), channel_id=1, source_target_pairs={{0,8},{4,12},{8,0},{12,4},{16,24},{20,28},{24,16},{28,20},{1,9},{5... | collective-permute-start | bytes 147464 | tf_op jit(solution)/shard_map/ppermute | solution.py:455
  11.8 5.0 %collective-permute-start.2 = (f32[2,32,128]{2,1,0:T(8,128)S(1)}, f32[2,32,128]{2,1,0:T(8,128)S(1)}, u32[]{:S(2)}, u32[]{:S(2)}) collective-permute-start(f32[2,32,128]{2,1,0:T(8,128)S(1)} %get-tuple-element.31.refs_4_), channel_id=1, source_target_pairs={{0,16},{4,20},{8,24},{12,28},{16,0},{20,4},{24,8},{28,12},{1,17},{... | collective-permute-start | bytes 98312 | tf_op jit(solution)/shard_map/ppermute | solution.py:455
  17.0 4.1 %collective-permute-start.3 = (f32[2,32,128]{2,1,0:T(8,128)S(1)}, f32[2,32,128]{2,1,0:T(8,128)S(1)}, u32[]{:S(2)}, u32[]{:S(2)}) collective-permute-start(f32[2,32,128]{2,1,0:T(8,128)S(1)} %get-tuple-element.35), channel_id=1, source_target_pairs={{0,1},{1,2},{2,3},{3,0},{4,5},{5,6},{6,7},{7,4},{8,9},{9,10},{10,1... | collective-permute-start | bytes 98312 | tf_op jit(solution)/shard_map/ppermute | solution.py:506
  17.0 4.0 %collective-permute-start.4 = (f32[2,32,128]{2,1,0:T(8,128)S(1)}, f32[2,32,128]{2,1,0:T(8,128)S(1)}, u32[]{:S(2)}, u32[]{:S(2)}) collective-permute-start(f32[2,32,128]{2,1,0:T(8,128)S(1)} %get-tuple-element.36), channel_id=1, source_target_pairs={{0,2},{1,3},{2,0},{3,1},{4,6},{5,7},{6,4},{7,5},{8,10},{9,11},{10,... | collective-permute-start | bytes 98312 | tf_op jit(solution)/shard_map/ppermute | solution.py:506
  18.9 3.0 %collective-permute-start.5 = (f32[2,32,128]{2,1,0:T(8,128)S(1)}, f32[2,32,128]{2,1,0:T(8,128)S(1)}, u32[]{:S(2)}, u32[]{:S(2)}) collective-permute-start(f32[2,32,128]{2,1,0:T(8,128)S(1)} %get-tuple-element.37), channel_id=1, source_target_pairs={{0,3},{1,0},{2,1},{3,2},{4,7},{5,4},{6,5},{7,6},{8,11},{9,8},{10,9... | collective-permute-start | bytes 98312 | tf_op jit(solution)/shard_map/ppermute | solution.py:506

commit v6 on v5

--- a/solution.py
+++ b/solution.py
@@ -14,7 +14,7 @@
 BF16 = jnp.bfloat16
 VMEM = 24 * 1024 * 1024
 FETCH_VMEM = 50 * 1024 * 1024
-CUTS = (0, 2, 5, 10, 16)
+CUTS = (0, 1, 3, 6, 11, 16)
 
 
 def down_sublanes(rates, lanes):

time: 23.6 us -> 23.6 us (level)
  no operation moved by 1% of the time
where the time goes in v6:
time: 23.6 us; the launch traced here: 23.5 us
  starting transfers between devices  11.6 us (49%)
  Pallas kernels  10.4 us (44%)
  waiting for transfers between devices  1.37 us (6%)
    ppermute x3, starting transfers between devices, per_device(): got = lax.ppermute(send, 'gy', [(i, i ^ 1 << stage) for i in range(dev_y)])  8.27 us
    pallas_call x3, Pallas kernels, per_device(): pl.pallas_call(functools.partial(local_kernel, dev_y, dev_z, lo, hi), in_...  5.65 us
    ppermute x3, starting transfers between devices, per_device(): lax.ppermute(send, 'gz', [(i, (i + by + 1) % dev_z) for i in range(dev_z)])  3.31 us
    pallas_call x1, Pallas kernels, per_device(): pl.pallas_call(functools.partial(final_kernel, dev_z, bounds), in_specs=[...  1.6 us
    pallas_call x1, Pallas kernels, per_device(): pl.pallas_call(fetch_kernel, in_specs=[hbm], out_specs=whole, out_shape=s...  1.57 us
    ppermute x3, waiting for transfers between devices, per_device(): lax.ppermute(send, 'gz', [(i, (i + by + 1) % dev_z) for i in range(dev_z)])  0.83 us
    pallas_call x1, Pallas kernels, per_device(): pl.pallas_call(functools.partial(held_kernel, stages - 1, dev_z), in_spec...  0.74 us
    pallas_call x1, Pallas kernels, per_device(): pl.pallas_call(functools.partial(moments_kernel, dev_y), in_specs=[whole,...  0.61 us
  transfers between devices with their start and end apart: 6, of which 3 were waited for; matrix products, arithmetic and copies ran while one was open for 0% of the time, Pallas kernels for 27%

profile of v6, /device:TPU:0, one launch (start us, length us, event | category | flops | bytes accessed | tf_op | source)
XLA Modules:
  0.0 23.5 jit_solution(15645486188337617485)
XLA Ops:
  0.0 0.0 copy-start
  0.0 1.6 %fetch.1.x.refs_2_.refs_0_ = f32[32,128,128]{2,1,0:T(8,128)S(1)} custom-call(f32[32,128,128]{2,1,0:T(8,128)} %x_hbm.1), custom_call_target="tpu_custom_call" | custom-call | flops 4 | bytes 4194304 | tf_op jit(solution)/shard_map/fetch/pallas_call | solution.py:425
  1.6 0.0 copy-done
  1.6 0.0 copy-start.1
  1.6 0.6 %moments.1.mine = f32[4,32,128]{2,1,0:T(8,128)S(1)} custom-call(f32[32]{0:T(128)S(1)} %copy-done, f32[32,128,128]{2,1,0:T(8,128)S(1)} %fetch.1.x.refs_2_.refs_0_), custom_call_target="tpu_custom_call" | custom-call | flops 2097152 | bytes 2097152 | tf_op jit(solution)/shard_map/moments/pallas_call | solution.py:435
  2.2 3.0 %collective-permute-start = (f32[4,32,128]{2,1,0:T(8,128)S(1)}, f32[4,32,128]{2,1,0:T(8,128)S(1)}, u32[]{:S(2)}, u32[]{:S(2)}) collective-permute-start(f32[4,32,128]{2,1,0:T(8,128)S(1)} %moments.1.mine), channel_id=1, source_target_pairs={{0,4},{4,0},{8,12},{12,8},{16,20},{20,16},{24,28},{28,24},{1,5},{5... | collective-permute-start | bytes 196616 | tf_op jit(solution)/shard_map/ppermute | solution.py:455
  5.3 0.0 copy-done.1
  5.3 1.9 %local.3 = (f32[10,128,128]{2,1,0:T(8,128)S(1)}, f32[10,8,128]{2,1,0:T(8,128)S(1)}, f32[5,32,128]{2,1,0:T(8,128)S(1)}, f32[7,32,128]{2,1,0:T(8,128)S(1)}, f32[7,...) custom-call(f32[32]{0:T(128)S(1)} %copy-done, f32[32]{0:T(128)S(1)} %copy-done.1, ...), custom_call_target="tpu_custom_call" | custom-call | flops 251658240 | bytes 1310720 | tf_op jit(solution)/shard_map/local/pallas_call | solution.py:471
  7.1 0.4 %collective-permute-done.got = f32[4,32,128]{2,1,0:T(8,128)S(1)} collective-permute-done((f32[4,32,128]{2,1,0:T(8,128)S(1)}, f32[4,32,128]{2,1,0:T(8,128)S(1)}, u32[]{:S(2)}, u32[]{:S(2)}) %collective-permute-start) | collective-permute-done | bytes 65568 | tf_op jit(solution)/shard_map/ppermute | solution.py:455
  7.5 2.1 %collective-permute-start.1 = (f32[3,32,128]{2,1,0:T(8,128)S(1)}, f32[3,32,128]{2,1,0:T(8,128)S(1)}, u32[]{:S(2)}, u32[]{:S(2)}) collective-permute-start(f32[3,32,128]{2,1,0:T(8,128)S(1)} %get-tuple-element.25.refs_4_.mine), channel_id=1, source_target_pairs={{0,8},{4,12},{8,0},{12,4},{16,24},{20,28},{24,16},{28,20},{1,9},{5... | collective-permute-start | bytes 147464 | tf_op jit(solution)/shard_map/ppermute | solution.py:455
  9.7 1.9 %local.4 = (f32[11,128,128]{2,1,0:T(8,128)S(1)}, f32[11,8,128]{2,1,0:T(8,128)S(1)}) custom-call(f32[32,128,128]{2,1,0:T(8,128)S(1)} %fetch.1.x.refs_2_.refs_0_, f32[7,32,128]{2,1,0:T(8,128)S(1)} %get-tuple-element.27.refs_1_, f32[8,32,128]{2,1,0:T(8,128)S(1)} %get-tuple-element.28.refs_2_, f32[32,8,128]{2,1,0:T(8,128)S(1)} %get-tuple-element.29.refs_3_, ...), custom_call_target="tpu_custom_call" | custom-call | flops 276824064 | bytes 1441792 | tf_op jit(solution)/shard_map/local/pallas_call | solution.py:471
  11.6 0.2 collective-permute-done.1.got
  11.8 3.1 %collective-permute-start.2 = (f32[2,32,128]{2,1,0:T(8,128)S(1)}, f32[2,32,128]{2,1,0:T(8,128)S(1)}, u32[]{:S(2)}, u32[]{:S(2)}) collective-permute-start(f32[2,32,128]{2,1,0:T(8,128)S(1)} %get-tuple-element.31.refs_4_), channel_id=1, source_target_pairs={{0,16},{4,20},{8,24},{12,28},{16,0},{20,4},{24,8},{28,12},{1,17},{... | collective-permute-start | bytes 98312 | tf_op jit(solution)/shard_map/ppermute | solution.py:455
  14.9 1.9 %local.5 = (f32[11,128,128]{2,1,0:T(8,128)S(1)}, f32[11,8,128]{2,1,0:T(8,128)S(1)}) custom-call(f32[32,128,128]{2,1,0:T(8,128)S(1)} %fetch.1.x.refs_2_.refs_0_, f32[7,32,128]{2,1,0:T(8,128)S(1)} %get-tuple-element.27.refs_1_, f32[8,32,128]{2,1,0:T(8,128)S(1)} %get-tuple-element.28.refs_2_, f32[32,8,128]{2,1,0:T(8,128)S(1)} %get-tuple-element.29.refs_3_, ...), custom_call_target="tpu_custom_call" | custom-call | flops 276824064 | bytes 1441792 | tf_op jit(solution)/shard_map/local/pallas_call | solution.py:471
  16.8 0.0 collective-permute-done.2.got
  16.8 0.2 middle.1
  17.0 0.1 collective-permute-start.3
  17.0 1.9 %collective-permute-start.4 = (f32[2,32,128]{2,1,0:T(8,128)S(1)}, f32[2,32,128]{2,1,0:T(8,128)S(1)}, u32[]{:S(2)}, u32[]{:S(2)}) collective-permute-start(f32[2,32,128]{2,1,0:T(8,128)S(1)} %get-tuple-element.36), channel_id=1, source_target_pairs={{0,2},{1,3},{2,0},{3,1},{4,6},{5,7},{6,4},{7,5},{8,10},{9,11},{10,... | collective-permute-start | bytes 98312 | tf_op jit(solution)/shard_map/ppermute | solution.py:506
  18.9 1.4 %collective-permute-start.5 = (f32[2,32,128]{2,1,0:T(8,128)S(1)}, f32[2,32,128]{2,1,0:T(8,128)S(1)}, u32[]{:S(2)}, u32[]{:S(2)}) collective-permute-start(f32[2,32,128]{2,1,0:T(8,128)S(1)} %get-tuple-element.37), channel_id=1, source_target_pairs={{0,3},{1,0},{2,1},{3,2},{4,7},{5,4},{6,5},{7,6},{8,11},{9,8},{10,9... | collective-permute-start | bytes 98312 | tf_op jit(solution)/shard_map/ppermute | solution.py:506
  20.3 0.7 %held.1.right = bf16[32,32,128]{2,1,0:T(8,128)(2,1)S(1)} custom-call(f32[32]{0:T(128)S(1)} %copy-done.1, f32[2,32,128]{2,1,0:T(8,128)S(1)} %collective-permute-done.2.got, f32[4,32,128]{2,1,0:T(8,128)S(1)} %get-tuple-element.32.held_in, f32[5,32,128]{2,1,0:T(8,128)S(1)} %get-tuple-element.23.refs_0_.refs_1_.ykeep, f32[7,32,128]{2,1,0:T(8,128)S(1)} %get-tuple-element.33.zkeep), custom_call_target="tpu_custom_call" | custom-call | flops 1638400 | bytes 409600 | tf_op jit(solution)/shard_map/held/pallas_call | solution.py:509
  21.0 0.0 collective-permute-done.3.rest_0_
  21.1 0.0 collective-permute-done.4.rest_1_
  21.1 0.8 %collective-permute-done.5.rest_2_ = f32[2,32,128]{2,1,0:T(8,128)S(1)} collective-permute-done((f32[2,32,128]{2,1,0:T(8,128)S(1)}, f32[2,32,128]{2,1,0:T(8,128)S(1)}, u32[]{:S(2)}, u32[]{:S(2)}) %collective-permute-start.5) | collective-permute-done | bytes 32800 | tf_op jit(solution)/shard_map/ppermute | solution.py:506
  21.9 1.6 %final.1 = f32[32,128,128]{2,1,0:T(8,128)} custom-call(bf16[32,32,128]{2,1,0:T(8,128)(2,1)S(1)} %held.1.right, f32[5,32,128]{2,1,0:T(8,128)S(1)} %get-tuple-element.23.refs_0_.refs_1_.ykeep, f32[7,32,128]{2,1,0:T(8,128)S(1)} %get-tuple-element.33.zkeep, f32[2,32,128]{2,1,0:T(8,128)S(1)} %collective-permute-done.3.rest_0_, ...), custom_call_target="tpu_custom_call" | custom-call | flops 33554432 | bytes 4194304 | tf_op jit(solution)/shard_map/final/pallas_call | solution.py:519
  (2 shorter events, 0.1 us)
Async XLA Ops:
  0.0 1.6 %copy-start = (f32[32]{0:T(128)S(1)}, f32[32]{0:T(128)}, u32[]{:S(2)}) copy-start(f32[32]{0:T(128)} %refs_0_.1) | copy-start | bytes 388
  1.6 3.7 %copy-start.1 = (f32[32]{0:T(128)S(1)}, f32[32]{0:T(128)}, u32[]{:S(2)}) copy-start(f32[32]{0:T(128)} %rates_z.1) | copy-start | bytes 388
  2.2 5.3 %collective-permute-start = (f32[4,32,128]{2,1,0:T(8,128)S(1)}, f32[4,32,128]{2,1,0:T(8,128)S(1)}, u32[]{:S(2)}, u32[]{:S(2)}) collective-permute-start(f32[4,32,128]{2,1,0:T(8,128)S(1)} %moments.1.mine), channel_id=1, source_target_pairs={{0,4},{4,0},{8,12},{12,8},{16,20},{20,16},{24,28},{28,24},{1,5},{5... | collective-permute-start | bytes 196616 | tf_op jit(solution)/shard_map/ppermute | solution.py:455
  7.5 4.2 %collective-permute-start.1 = (f32[3,32,128]{2,1,0:T(8,128)S(1)}, f32[3,32,128]{2,1,0:T(8,128)S(1)}, u32[]{:S(2)}, u32[]{:S(2)}) collective-permute-start(f32[3,32,128]{2,1,0:T(8,128)S(1)} %get-tuple-element.25.refs_4_.mine), channel_id=1, source_target_pairs={{0,8},{4,12},{8,0},{12,4},{16,24},{20,28},{24,16},{28,20},{1,9},{5... | collective-permute-start | bytes 147464 | tf_op jit(solution)/shard_map/ppermute | solution.py:455
  11.8 5.0 %collective-permute-start.2 = (f32[2,32,128]{2,1,0:T(8,128)S(1)}, f32[2,32,128]{2,1,0:T(8,128)S(1)}, u32[]{:S(2)}, u32[]{:S(2)}) collective-permute-start(f32[2,32,128]{2,1,0:T(8,128)S(1)} %get-tuple-element.31.refs_4_), channel_id=1, source_target_pairs={{0,16},{4,20},{8,24},{12,28},{16,0},{20,4},{24,8},{28,12},{1,17},{... | collective-permute-start | bytes 98312 | tf_op jit(solution)/shard_map/ppermute | solution.py:455
  17.0 4.1 %collective-permute-start.3 = (f32[2,32,128]{2,1,0:T(8,128)S(1)}, f32[2,32,128]{2,1,0:T(8,128)S(1)}, u32[]{:S(2)}, u32[]{:S(2)}) collective-permute-start(f32[2,32,128]{2,1,0:T(8,128)S(1)} %get-tuple-element.35), channel_id=1, source_target_pairs={{0,1},{1,2},{2,3},{3,0},{4,5},{5,6},{6,7},{7,4},{8,9},{9,10},{10,1... | collective-permute-start | bytes 98312 | tf_op jit(solution)/shard_map/ppermute | solution.py:506
  17.0 4.0 %collective-permute-start.4 = (f32[2,32,128]{2,1,0:T(8,128)S(1)}, f32[2,32,128]{2,1,0:T(8,128)S(1)}, u32[]{:S(2)}, u32[]{:S(2)}) collective-permute-start(f32[2,32,128]{2,1,0:T(8,128)S(1)} %get-tuple-element.36), channel_id=1, source_target_pairs={{0,2},{1,3},{2,0},{3,1},{4,6},{5,7},{6,4},{7,5},{8,10},{9,11},{10,... | collective-permute-start | bytes 98312 | tf_op jit(solution)/shard_map/ppermute | solution.py:506
  18.9 3.0 %collective-permute-start.5 = (f32[2,32,128]{2,1,0:T(8,128)S(1)}, f32[2,32,128]{2,1,0:T(8,128)S(1)}, u32[]{:S(2)}, u32[]{:S(2)}) collective-permute-start(f32[2,32,128]{2,1,0:T(8,128)S(1)} %get-tuple-element.37), channel_id=1, source_target_pairs={{0,3},{1,0},{2,1},{3,2},{4,7},{5,4},{6,5},{7,6},{8,11},{9,8},{10,9... | collective-permute-start | bytes 98312 | tf_op jit(solution)/shard_map/ppermute | solution.py:506
